TPU v7x, 32 devices: a whole 2x2x4 slice. The times are simulated.
32 devices in a mesh: seq: 16 (over z, y, core), head: 2 (over x).
Axes of the slice: x: 2, y: 2, z: 4, core: 2. Of those that a mesh axis runs over, the one named last changes fastest.
Arguments:
- queries: bfloat16 [2048, 3072], P('seq', 'head'), may hold values from -6 to 6
- keys: bfloat16 [2048, 3072], P('seq', 'head'), may hold values from -6 to 6
- values: bfloat16 [2048, 3072], P('seq', 'head'), may hold values from -6 to 6
- cache_k: bfloat16 [2048, 3072], P('seq', 'head'), may hold values from -6 to 6
- cache_v: bfloat16 [2048, 3072], P('seq', 'head'), may hold values from -6 to 6
- sink_k: bfloat16 [8, 3072], P(None, 'head'), may hold values from -6 to 6
- sink_v: bfloat16 [8, 3072], P(None, 'head'), may hold values from -6 to 6
- suffix_lengths: int32 [4], replicated, may hold values from 1 to 1024, 2048 in all
- request_group: int32 [4], replicated, may hold values from 0 to 1
- w_out: bfloat16 [3072, 3072], P('head'), may hold values from -0.109375 to 0.109375
Outputs:
- projected: bfloat16 [3072, 2048], P('head', 'seq')
All inputs are finite; a program needn't handle non-finite values.
Results may differ from a plain program's by a relative error of at most 0.011.
Values may be sent and summed in bfloat16 or wider, within the bound.
A program may use at most 128 MiB of HBM per device.

v0:
```python
import math

import jax
import jax.numpy as jnp
from jax import lax
from jax.sharding import PartitionSpec as P

HD = 96
W = 1024
SINKS = 4


def from_behind(array, axis, by):
    devices = lax.axis_size(axis)
    pairs = [(i, i + by) for i in range(devices) if 0 <= i + by < devices]
    return lax.ppermute(array, axis, pairs)


def describe(index, starts, lengths, groups):
    inside = (starts[None, :] <= index[:, None]) & (index[:, None] < (starts + lengths)[None, :])
    flag = inside.astype(jnp.int32)
    found = jnp.sum(flag, axis=1)
    request = jnp.sum(flag * jnp.arange(starts.shape[0], dtype=jnp.int32)[None, :], axis=1)
    request = jnp.where(found > 0, request, -1)
    offset = index - jnp.sum(flag * starts[None, :], axis=1)
    group = jnp.sum(flag * groups[None, :], axis=1)
    return (request, offset, group)


def shards(
    queries, keys, values, cache_k, cache_v, sink_k, sink_v, suffix_lengths, request_group, w_out
):
    rows, width = queries.shape
    heads = width // HD
    scale = 1.0 / math.sqrt(HD)
    device = lax.axis_index("seq")
    starts = jnp.cumsum(suffix_lengths) - suffix_lengths
    index = device * rows + jnp.arange(rows, dtype=jnp.int32)
    req_q, off_q, grp_q = describe(index, starts, suffix_lengths, request_group)
    q_three = queries.reshape(rows, heads, HD)

    def absorb(state, key_rows, value_rows, mask):
        top, den, acc = state
        count = key_rows.shape[0]
        k_three = key_rows.reshape(count, heads, HD)
        v_three = value_rows.reshape(count, heads, HD)
        score = (
            jnp.einsum("shd,khd->hsk", q_three, k_three, preferred_element_type=jnp.float32) * scale
        )
        score = jnp.where(mask[None], score, jnp.float32(-1e30))
        new_top = jnp.maximum(top, jnp.max(score, axis=2))
        factor = jnp.exp(top - new_top)
        prob = jnp.where(mask[None], jnp.exp(score - new_top[:, :, None]), jnp.float32(0.0))
        den = den * factor + jnp.sum(prob, axis=2)
        part = jnp.einsum(
            "hsk,khd->hsd", prob.astype(jnp.bfloat16), v_three, preferred_element_type=jnp.float32
        )
        acc = acc * factor[:, :, None] + part
        return (new_top, den, acc)

    def suffix_mask(near):
        req_k, off_k, grp_k = describe(near, starts, suffix_lengths, request_group)
        return (
            (req_k[None, :] == req_q[:, None])
            & (near[None, :] <= index[:, None])
            & (index[:, None] - near[None, :] < W)
            & (near[None, :] >= 0)
        )

    state = (
        jnp.full((heads, rows), -1e30, jnp.float32),
        jnp.zeros((heads, rows), jnp.float32),
        jnp.zeros((heads, rows, HD), jnp.float32),
    )
    sink_group = jnp.arange(sink_k.shape[0], dtype=jnp.int32) // SINKS
    state = absorb(state, sink_k, sink_v, grp_q[:, None] == sink_group[None, :])
    pieces = (
        lax.all_gather(cache_k, "seq", axis=0, tiled=True),
        lax.all_gather(cache_v, "seq", axis=0, tiled=True),
    )
    slot = jnp.arange(pieces[0].shape[0], dtype=jnp.int32)
    state = absorb(
        state,
        pieces[0],
        pieces[1],
        (grp_q[:, None] == (slot // W)[None, :]) & ((slot % W)[None, :] > off_q[:, None]),
    )
    state = absorb(state, keys, values, suffix_mask(index))
    reach = W // rows
    current = (keys, values)
    for step in range(1, reach + 1):
        current = from_behind((current[0], current[1]), "seq", 1)
        near = (device - step) * rows + jnp.arange(rows, dtype=jnp.int32)
        state = absorb(state, current[0], current[1], suffix_mask(near))
    top, den, acc = state
    attn = (acc / den[:, :, None]).transpose(1, 0, 2).reshape(rows, width).astype(jnp.bfloat16)
    return lax.psum_scatter(
        jnp.einsum("cd,sc->ds", w_out, attn, preferred_element_type=jnp.float32).astype(
            jnp.bfloat16
        ),
        "head",
        scatter_dimension=0,
        tiled=True,
    )


def solution(mesh):
    placed = (
        P("seq", "head"),
        P("seq", "head"),
        P("seq", "head"),
        P("seq", "head"),
        P("seq", "head"),
        P(None, "head"),
        P(None, "head"),
        P(),
        P(),
        P("head", None),
    )
    return jax.shard_map(
        shards, mesh=mesh, in_specs=placed, out_specs=P("head", "seq"), check_vma=False
    )
```

profile of v0, /device:TPU:0, one launch (start us, length us, event | category | flops | bytes accessed | tf_op | source)
XLA Modules:
  0.0 252.7 jit_solution(2121656940890473196)
XLA Ops:
  6.5 0.7 all-gather.3.cloned.1.call-update
  8.1 2.4 collective-permute-start
  10.4 4.5 %collective-permute-start.1 = (bf16[128,1536]{1,0:T(8,128)(2,1)}, bf16[128,1536]{1,0:T(8,128)(2,1)S(1)}, u32[]{:S(2)}, u32[]{:S(2)}) collective-permute-start(bf16[128,1536]{1,0:T(8,128)(2,1)} %param.12), channel_id=1, source_target_pairs={{0,2},{2,4},{4,6},{6,8},{8,10},{10,12},{12,14},{14,16},{16,18},{18... | collective-permute-start | bytes 1179656 | tf_op jit(solution)/shard_map/ppermute | solution.py:16
  15.0 0.8 reduce-window.8
  16.8 0.7 convert_reduce_fusion.8
  17.7 1.1 fusion.98
  18.9 2.6 %collective-permute-start.2 = (bf16[128,1536]{1,0:T(8,128)(2,1)S(1)}, bf16[128,1536]{1,0:T(8,128)(2,1)}, u32[]{:S(2)}, u32[]{:S(2)}) collective-permute-start(bf16[128,1536]{1,0:T(8,128)(2,1)S(1)} %collective-permute-done), channel_id=1, source_target_pairs={{0,2},{2,4},{4,6},{6,8},{8,10},{10,12},{12,14},{14,16},{16,18},{18... | collective-permute-start | bytes 1179656 | tf_op jit(solution)/shard_map/ppermute | solution.py:16
  21.5 4.8 %collective-permute-start.3 = (bf16[128,1536]{1,0:T(8,128)(2,1)S(1)}, bf16[128,1536]{1,0:T(8,128)(2,1)S(1)}, u32[]{:S(2)}, u32[]{:S(2)}) collective-permute-start(bf16[128,1536]{1,0:T(8,128)(2,1)S(1)} %collective-permute-done.1), channel_id=1, source_target_pairs={{0,2},{2,4},{4,6},{6,8},{8,10},{10,12},{12,14},{14,16},{16,18},{18... | collective-permute-start | bytes 1179656 | tf_op jit(solution)/shard_map/ppermute | solution.py:16
  26.3 1.2 copy.87
  27.5 0.8 reshape.1639
  28.4 1.4 fusion.171
  29.8 5.0 %collective-permute-start.4 = (bf16[128,1536]{1,0:T(8,128)(2,1)}, bf16[128,1536]{1,0:T(8,128)(2,1)}, u32[]{:S(2)}, u32[]{:S(2)}) collective-permute-start(bf16[128,1536]{1,0:T(8,128)(2,1)} %collective-permute-done.2), channel_id=1, source_target_pairs={{0,2},{2,4},{4,6},{6,8},{8,10},{10,12},{12,14},{14,16},{16,18},{18... | collective-permute-start | bytes 1179656 | tf_op jit(solution)/shard_map/ppermute | solution.py:16
  34.9 2.9 %collective-permute-start.5 = (bf16[128,1536]{1,0:T(8,128)(2,1)S(1)}, bf16[128,1536]{1,0:T(8,128)(2,1)}, u32[]{:S(2)}, u32[]{:S(2)}) collective-permute-start(bf16[128,1536]{1,0:T(8,128)(2,1)S(1)} %collective-permute-done.3), channel_id=1, source_target_pairs={{0,2},{2,4},{4,6},{6,8},{8,10},{10,12},{12,14},{14,16},{16,18},{18... | collective-permute-start | bytes 1179656 | tf_op jit(solution)/shard_map/ppermute | solution.py:16
  37.8 1.2 copy.92
  39.0 1.9 copy.93
  40.9 1.4 reshape.1640
  42.4 1.0 fusion.170
  43.3 6.7 %collective-permute-start.6 = (bf16[128,1536]{1,0:T(8,128)(2,1)}, bf16[128,1536]{1,0:T(8,128)(2,1)}, u32[]{:S(2)}, u32[]{:S(2)}) collective-permute-start(bf16[128,1536]{1,0:T(8,128)(2,1)} %collective-permute-done.4), channel_id=1, source_target_pairs={{0,2},{2,4},{4,6},{6,8},{8,10},{10,12},{12,14},{14,16},{16,18},{18... | collective-permute-start | bytes 1179656 | tf_op jit(solution)/shard_map/ppermute | solution.py:16
  50.0 7.0 %collective-permute-start.7 = (bf16[128,1536]{1,0:T(8,128)(2,1)}, bf16[128,1536]{1,0:T(8,128)(2,1)}, u32[]{:S(2)}, u32[]{:S(2)}) collective-permute-start(bf16[128,1536]{1,0:T(8,128)(2,1)} %collective-permute-done.5), channel_id=1, source_target_pairs={{0,2},{2,4},{4,6},{6,8},{8,10},{10,12},{12,14},{14,16},{16,18},{18... | collective-permute-start | bytes 1179656 | tf_op jit(solution)/shard_map/ppermute | solution.py:16
  57.1 1.0 compare_and_fusion
  58.0 12.4 %collective-permute-start.8 = (bf16[128,1536]{1,0:T(8,128)(2,1)}, bf16[128,1536]{1,0:T(8,128)(2,1)}, u32[]{:S(2)}, u32[]{:S(2)}) collective-permute-start(bf16[128,1536]{1,0:T(8,128)(2,1)} %collective-permute-done.6), channel_id=1, source_target_pairs={{0,2},{2,4},{4,6},{6,8},{8,10},{10,12},{12,14},{14,16},{16,18},{18... | collective-permute-start | bytes 1179656 | tf_op jit(solution)/shard_map/ppermute | solution.py:16
  70.4 4.3 %collective-permute-start.9 = (bf16[128,1536]{1,0:T(8,128)(2,1)}, bf16[128,1536]{1,0:T(8,128)(2,1)}, u32[]{:S(2)}, u32[]{:S(2)}) collective-permute-start(bf16[128,1536]{1,0:T(8,128)(2,1)} %collective-permute-done.7), channel_id=1, source_target_pairs={{0,2},{2,4},{4,6},{6,8},{8,10},{10,12},{12,14},{14,16},{16,18},{18... | collective-permute-start | bytes 1179656 | tf_op jit(solution)/shard_map/ppermute | solution.py:16
  74.8 0.8 fusion.100
  75.8 1.0 copy.96
  76.8 1.0 fusion.169
  77.7 1.9 copy.98
  79.6 8.0 %collective-permute-start.10 = (bf16[128,1536]{1,0:T(8,128)(2,1)}, bf16[128,1536]{1,0:T(8,128)(2,1)}, u32[]{:S(2)}, u32[]{:S(2)}) collective-permute-start(bf16[128,1536]{1,0:T(8,128)(2,1)} %collective-permute-done.8), channel_id=1, source_target_pairs={{0,2},{2,4},{4,6},{6,8},{8,10},{10,12},{12,14},{14,16},{16,18},{18... | collective-permute-start | bytes 1179656 | tf_op jit(solution)/shard_map/ppermute | solution.py:16
  87.7 10.8 %collective-permute-start.11 = (bf16[128,1536]{1,0:T(8,128)(2,1)}, bf16[128,1536]{1,0:T(8,128)(2,1)}, u32[]{:S(2)}, u32[]{:S(2)}) collective-permute-start(bf16[128,1536]{1,0:T(8,128)(2,1)} %collective-permute-done.9), channel_id=1, source_target_pairs={{0,2},{2,4},{4,6},{6,8},{8,10},{10,12},{12,14},{14,16},{16,18},{18... | collective-permute-start | bytes 1179656 | tf_op jit(solution)/shard_map/ppermute | solution.py:16
  98.5 2.0 fusion.168
  100.5 1.9 copy.99
  102.4 1.9 copy.101
  104.3 1.9 copy.102
  106.2 3.0 %fusion.167 = (f32[16,128]{1,0:T(8,128)}, f32[16,128,128]{1,2,0:T(8,128)}) fusion(bf16[128,16,96]{0,2,1:T(8,128)(2,1)S(1)} %bitcast.297, bf16[128,16,96]{0,2,1:T(8,128)(2,1)} %bitcast.322, pred[128,128]{0,1:T(8,128)(4,1)} %get-tuple-element.55), kind=kOutput, calls=%fused_computation.293 | convolution fusion | flops 51116032 | bytes 1859584 | tf_op jit(solution)/shard_map/shd,khd->hsk/dot_general | solution.py:48
  109.2 1.9 copy.104
  111.1 5.3 %collective-permute-start.12 = (bf16[128,1536]{1,0:T(8,128)(2,1)}, bf16[128,1536]{1,0:T(8,128)(2,1)}, u32[]{:S(2)}, u32[]{:S(2)}) collective-permute-start(bf16[128,1536]{1,0:T(8,128)(2,1)} %collective-permute-done.10), channel_id=1, source_target_pairs={{0,2},{2,4},{4,6},{6,8},{8,10},{10,12},{12,14},{14,16},{16,18},{18... | collective-permute-start | bytes 1179656 | tf_op jit(solution)/shard_map/ppermute | solution.py:16
  116.4 2.1 collective-permute-start.13
  118.5 2.9 %fusion.166 = (f32[16,128]{1,0:T(8,128)}, f32[16,128,128]{1,2,0:T(8,128)}) fusion(bf16[128,16,96]{0,2,1:T(8,128)(2,1)S(1)} %bitcast.298, bf16[128,16,96]{0,2,1:T(8,128)(2,1)} %bitcast.317, pred[128,128]{0,1:T(8,128)(4,1)S(1)} %get-tuple-element.59), kind=kOutput, calls=%fused_computation.292 | convolution fusion | flops 51116032 | bytes 1859584 | tf_op jit(solution)/shard_map/shd,khd->hsk/dot_general | solution.py:48
  121.4 1.9 copy.105
  123.3 2.0 copy.107
  125.3 1.9 copy.108
  127.3 2.9 %fusion.165 = (f32[16,128]{1,0:T(8,128)}, f32[16,128,128]{1,2,0:T(8,128)}) fusion(bf16[128,16,96]{0,2,1:T(8,128)(2,1)S(1)} %bitcast.299, bf16[128,16,96]{0,2,1:T(8,128)(2,1)} %bitcast.323, pred[128,128]{0,1:T(8,128)(4,1)} %get-tuple-element.52), kind=kOutput, calls=%fused_computation.291 | convolution fusion | flops 51116032 | bytes 1859584 | tf_op jit(solution)/shard_map/shd,khd->hsk/dot_general | solution.py:48
  130.2 1.9 copy.110
  132.1 3.3 %collective-permute-start.14 = (bf16[128,1536]{1,0:T(8,128)(2,1)}, bf16[128,1536]{1,0:T(8,128)(2,1)}, u32[]{:S(2)}, u32[]{:S(2)}) collective-permute-start(bf16[128,1536]{1,0:T(8,128)(2,1)} %collective-permute-done.12), channel_id=1, source_target_pairs={{0,2},{2,4},{4,6},{6,8},{8,10},{10,12},{12,14},{14,16},{16,18},{18... | collective-permute-start | bytes 1179656 | tf_op jit(solution)/shard_map/ppermute | solution.py:16
  135.4 5.7 %collective-permute-start.15 = (bf16[128,1536]{1,0:T(8,128)(2,1)}, bf16[128,1536]{1,0:T(8,128)(2,1)}, u32[]{:S(2)}, u32[]{:S(2)}) collective-permute-start(bf16[128,1536]{1,0:T(8,128)(2,1)} %collective-permute-done.13), channel_id=1, source_target_pairs={{0,2},{2,4},{4,6},{6,8},{8,10},{10,12},{12,14},{14,16},{16,18},{18... | collective-permute-start | bytes 1179656 | tf_op jit(solution)/shard_map/ppermute | solution.py:16
  141.1 3.0 %fusion.164 = (f32[16,128]{1,0:T(8,128)}, f32[16,128,128]{1,2,0:T(8,128)}) fusion(bf16[128,16,96]{0,2,1:T(8,128)(2,1)S(1)} %bitcast.300, bf16[128,16,96]{0,2,1:T(8,128)(2,1)} %bitcast.318, pred[128,128]{0,1:T(8,128)(4,1)} %get-tuple-element.56), kind=kOutput, calls=%fused_computation.290 | convolution fusion | flops 51116032 | bytes 1859584 | tf_op jit(solution)/shard_map/shd,khd->hsk/dot_general | solution.py:48
  144.1 1.9 copy.111
  146.0 1.9 copy.113
  147.9 1.9 copy.114
  149.8 2.9 %fusion.163 = (f32[16,128]{1,0:T(8,128)}, f32[16,128,128]{1,2,0:T(8,128)}) fusion(bf16[128,16,96]{0,2,1:T(8,128)(2,1)S(1)} %bitcast.301, bf16[128,16,96]{0,2,1:T(8,128)(2,1)} %bitcast.324, pred[128,128]{0,1:T(8,128)(4,1)} %get-tuple-element.54), kind=kOutput, calls=%fused_computation.289 | convolution fusion | flops 51116032 | bytes 1859584 | tf_op jit(solution)/shard_map/shd,khd->hsk/dot_general | solution.py:48
  152.8 1.9 copy.116
  154.7 2.0 copy.117
  156.7 3.0 %fusion.162 = (f32[16,128]{1,0:T(8,128)}, f32[16,128,128]{1,2,0:T(8,128)}) fusion(bf16[128,16,96]{0,2,1:T(8,128)(2,1)S(1)} %bitcast.302, bf16[128,16,96]{0,2,1:T(8,128)(2,1)} %bitcast.319, pred[128,128]{0,1:T(8,128)(4,1)} %get-tuple-element.58), kind=kOutput, calls=%fused_computation.288 | convolution fusion | flops 51116032 | bytes 1859584 | tf_op jit(solution)/shard_map/shd,khd->hsk/dot_general | solution.py:48
  159.7 8.7 %copy.90 = bf16[2048,1536]{0,1:T(8,128)(2,1)} copy(bf16[2048,1536]{1,0:T(8,128)(2,1)} %all-gather.3.cloned.1.call-done) | data formatting | bytes 12582912 | tf_op jit(solution)/shard_map/all_gather | solution.py:78
  168.4 5.7 %fusion = (f32[16,128]{1,0:T(8,128)S(1)}, f32[16,128,2048]{2,1,0:T(8,128)S(1)}) fusion(pred[128,2048]{1,0:T(8,128)(4,1)} %compare_and_fusion, bf16[128,16,96]{0,2,1:T(8,128)(2,1)S(1)} %bitcast.303, bf16[2048,16,96]{0,2,1:T(8,128)(2,1)} %bitcast.304), kind=kOutput, calls=%fused_computation.2 | convolution fusion | flops 817887232 | bytes 23732224 | tf_op jit(solution)/shard_map/shd,khd->hsk/dot_general | solution.py:48
  175.5 4.4 %copy-done = f32[16,128,2048]{2,1,0:T(8,128)} copy-done((f32[16,128,2048]{2,1,0:T(8,128)}, f32[16,128,2048]{2,1,0:T(8,128)S(1)}, u32[]{:S(2)}) %copy-start) | copy-done | bytes 16777240
  179.9 5.6 %fusion.1 = f32[16,128]{1,0:T(8,128)} fusion(f32[16,128,2048]{2,1,0:T(8,128)S(1)} %get-tuple-element.88, f32[16,128]{1,0:T(8,128)S(1)} %get-tuple-element.44, pred[128,2048]{1,0:T(8,128)(4,1)S(1)} %copy-done.6), kind=kLoop, calls=%fused_computation.3 | loop fusion | flops 20969472 | bytes 17055744 | tf_op jit(solution)/shard_map/reduce_sum | solution.py:54
  185.5 8.7 %copy.91 = bf16[2048,1536]{0,1:T(8,128)(2,1)} copy(bf16[2048,1536]{1,0:T(8,128)(2,1)} %all-gather.5.cloned.1.call-done) | data formatting | bytes 12582912 | tf_op jit(solution)/shard_map/all_gather | solution.py:79
  194.5 10.3 %fusion.38 = f32[128,16,96]{0,2,1:T(8,128)S(1)} fusion(bf16[2048,16,96]{0,2,1:T(8,128)(2,1)} %bitcast.307, f32[16,128,2048]{2,1,0:T(8,128)} %copy-done, f32[16,128]{1,0:T(8,128)} %copy-done.55, pred[128,2048]{1,0:T(8,128)(4,1)S(1)} %copy-done.7), kind=kOutput, calls=%fused_computation.59 | convolution fusion | flops 826277888 | bytes 24125440 | tf_op jit(solution)/shard_map/hsk,khd->hsd/dot_general | solution.py:55
  206.9 1.0 fusion.115
  207.9 0.9 bitcast_add_fusion
  208.8 1.1 fusion.37
  213.3 2.3 fusion.6
  215.6 28.6 %reduce-scatter.2.cloned.1.call-done = bf16[1536,128]{0,1:T(8,128)(2,1)} async-done(((bf16[3072,128]{0,1:T(8,128)(2,1)}), bf16[1536,128]{0,1:T(8,128)(2,1)}) %reduce-scatter.2.cloned.1.call-update) | async-done | bytes 393232 | tf_op jit(solution)/shard_map/reduce_scatter | solution.py:97
  244.2 1.9 copy.119
  (199 shorter events, 8.5 us)
Async XLA Ops:
  6.5 153.1 %all-gather.3.cloned.1.call-start = ((), (), s32[]{:S(2)}) async-start(), calls=%async_computation.1 | async-start | bytes 6684672 | tf_op jit(solution)/shard_map/all_gather | solution.py:78
  7.3 178.3 %all-gather.5.cloned.1.call-start = ((), (), s32[]{:S(2)}) async-start(), calls=%async_computation.2 | async-start | bytes 6684672 | tf_op jit(solution)/shard_map/all_gather | solution.py:79
  8.0 236.2 %reduce-scatter.2.cloned.1.call-start = ((), (), s32[]{:S(2)}) async-start(), calls=%async_computation.3 | async-start | bytes 1179648 | tf_op jit(solution)/shard_map/reduce_scatter | solution.py:97
  8.1 10.8 %collective-permute-start = (bf16[128,1536]{1,0:T(8,128)(2,1)}, bf16[128,1536]{1,0:T(8,128)(2,1)S(1)}, u32[]{:S(2)}, u32[]{:S(2)}) collective-permute-start(bf16[128,1536]{1,0:T(8,128)(2,1)} %param.11), channel_id=1, source_target_pairs={{0,2},{2,4},{4,6},{6,8},{8,10},{10,12},{12,14},{14,16},{16,18},{18... | collective-permute-start | bytes 1179656 | tf_op jit(solution)/shard_map/ppermute | solution.py:16
  10.4 11.1 %collective-permute-start.1 = (bf16[128,1536]{1,0:T(8,128)(2,1)}, bf16[128,1536]{1,0:T(8,128)(2,1)S(1)}, u32[]{:S(2)}, u32[]{:S(2)}) collective-permute-start(bf16[128,1536]{1,0:T(8,128)(2,1)} %param.12), channel_id=1, source_target_pairs={{0,2},{2,4},{4,6},{6,8},{8,10},{10,12},{12,14},{14,16},{16,18},{18... | collective-permute-start | bytes 1179656 | tf_op jit(solution)/shard_map/ppermute | solution.py:16
  17.7 57.1 %copy-start.57 = (pred[128,8]{0,1:T(8,128)(4,1)}, pred[128,8]{0,1:T(8,128)(4,1)S(1)}, u32[]{:S(2)}) copy-start(pred[128,8]{0,1:T(8,128)(4,1)S(1)} %broadcast_compare_fusion) | copy-start | bytes 3076
  18.8 55.9 %copy-start.27 = (pred[128,128]{0,1:T(8,128)(4,1)}, pred[128,128]{0,1:T(8,128)(4,1)S(1)}, u32[]{:S(2)}) copy-start(pred[128,128]{0,1:T(8,128)(4,1)S(1)} %get-tuple-element.51) | copy-start | bytes 49156
  18.9 11.0 %collective-permute-start.2 = (bf16[128,1536]{1,0:T(8,128)(2,1)S(1)}, bf16[128,1536]{1,0:T(8,128)(2,1)}, u32[]{:S(2)}, u32[]{:S(2)}) collective-permute-start(bf16[128,1536]{1,0:T(8,128)(2,1)S(1)} %collective-permute-done), channel_id=1, source_target_pairs={{0,2},{2,4},{4,6},{6,8},{8,10},{10,12},{12,14},{14,16},{16,18},{18... | collective-permute-start | bytes 1179656 | tf_op jit(solution)/shard_map/ppermute | solution.py:16
  21.5 13.4 %collective-permute-start.3 = (bf16[128,1536]{1,0:T(8,128)(2,1)S(1)}, bf16[128,1536]{1,0:T(8,128)(2,1)S(1)}, u32[]{:S(2)}, u32[]{:S(2)}) collective-permute-start(bf16[128,1536]{1,0:T(8,128)(2,1)S(1)} %collective-permute-done.1), channel_id=1, source_target_pairs={{0,2},{2,4},{4,6},{6,8},{8,10},{10,12},{12,14},{14,16},{16,18},{18... | collective-permute-start | bytes 1179656 | tf_op jit(solution)/shard_map/ppermute | solution.py:16
  29.8 13.5 %collective-permute-start.4 = (bf16[128,1536]{1,0:T(8,128)(2,1)}, bf16[128,1536]{1,0:T(8,128)(2,1)}, u32[]{:S(2)}, u32[]{:S(2)}) collective-permute-start(bf16[128,1536]{1,0:T(8,128)(2,1)} %collective-permute-done.2), channel_id=1, source_target_pairs={{0,2},{2,4},{4,6},{6,8},{8,10},{10,12},{12,14},{14,16},{16,18},{18... | collective-permute-start | bytes 1179656 | tf_op jit(solution)/shard_map/ppermute | solution.py:16
  34.9 39.9 %copy-start.19 = (bf16[128,1536]{1,0:T(8,128)(2,1)}, bf16[128,1536]{1,0:T(8,128)(2,1)S(1)}, u32[]{:S(2)}) copy-start(bf16[128,1536]{1,0:T(8,128)(2,1)S(1)} %collective-permute-done.3) | copy-start | bytes 1179652
  34.9 15.2 %collective-permute-start.5 = (bf16[128,1536]{1,0:T(8,128)(2,1)S(1)}, bf16[128,1536]{1,0:T(8,128)(2,1)}, u32[]{:S(2)}, u32[]{:S(2)}) collective-permute-start(bf16[128,1536]{1,0:T(8,128)(2,1)S(1)} %collective-permute-done.3), channel_id=1, source_target_pairs={{0,2},{2,4},{4,6},{6,8},{8,10},{10,12},{12,14},{14,16},{16,18},{18... | collective-permute-start | bytes 1179656 | tf_op jit(solution)/shard_map/ppermute | solution.py:16
  43.3 14.7 %collective-permute-start.6 = (bf16[128,1536]{1,0:T(8,128)(2,1)}, bf16[128,1536]{1,0:T(8,128)(2,1)}, u32[]{:S(2)}, u32[]{:S(2)}) collective-permute-start(bf16[128,1536]{1,0:T(8,128)(2,1)} %collective-permute-done.4), channel_id=1, source_target_pairs={{0,2},{2,4},{4,6},{6,8},{8,10},{10,12},{12,14},{14,16},{16,18},{18... | collective-permute-start | bytes 1179656 | tf_op jit(solution)/shard_map/ppermute | solution.py:16
  50.0 20.4 %collective-permute-start.7 = (bf16[128,1536]{1,0:T(8,128)(2,1)}, bf16[128,1536]{1,0:T(8,128)(2,1)}, u32[]{:S(2)}, u32[]{:S(2)}) collective-permute-start(bf16[128,1536]{1,0:T(8,128)(2,1)} %collective-permute-done.5), channel_id=1, source_target_pairs={{0,2},{2,4},{4,6},{6,8},{8,10},{10,12},{12,14},{14,16},{16,18},{18... | collective-permute-start | bytes 1179656 | tf_op jit(solution)/shard_map/ppermute | solution.py:16
  58.0 21.6 %collective-permute-start.8 = (bf16[128,1536]{1,0:T(8,128)(2,1)}, bf16[128,1536]{1,0:T(8,128)(2,1)}, u32[]{:S(2)}, u32[]{:S(2)}) collective-permute-start(bf16[128,1536]{1,0:T(8,128)(2,1)} %collective-permute-done.6), channel_id=1, source_target_pairs={{0,2},{2,4},{4,6},{6,8},{8,10},{10,12},{12,14},{14,16},{16,18},{18... | collective-permute-start | bytes 1179656 | tf_op jit(solution)/shard_map/ppermute | solution.py:16
  70.4 17.3 %collective-permute-start.9 = (bf16[128,1536]{1,0:T(8,128)(2,1)}, bf16[128,1536]{1,0:T(8,128)(2,1)}, u32[]{:S(2)}, u32[]{:S(2)}) collective-permute-start(bf16[128,1536]{1,0:T(8,128)(2,1)} %collective-permute-done.7), channel_id=1, source_target_pairs={{0,2},{2,4},{4,6},{6,8},{8,10},{10,12},{12,14},{14,16},{16,18},{18... | collective-permute-start | bytes 1179656 | tf_op jit(solution)/shard_map/ppermute | solution.py:16
  75.6 22.9 %copy-start.20 = (pred[128,128]{0,1:T(8,128)(4,1)}, pred[128,128]{0,1:T(8,128)(4,1)S(1)}, u32[]{:S(2)}) copy-start(pred[128,128]{0,1:T(8,128)(4,1)S(1)} %get-tuple-element.57) | copy-start | bytes 49156
  79.6 31.5 %collective-permute-start.10 = (bf16[128,1536]{1,0:T(8,128)(2,1)}, bf16[128,1536]{1,0:T(8,128)(2,1)}, u32[]{:S(2)}, u32[]{:S(2)}) collective-permute-start(bf16[128,1536]{1,0:T(8,128)(2,1)} %collective-permute-done.8), channel_id=1, source_target_pairs={{0,2},{2,4},{4,6},{6,8},{8,10},{10,12},{12,14},{14,16},{16,18},{18... | collective-permute-start | bytes 1179656 | tf_op jit(solution)/shard_map/ppermute | solution.py:16
  87.7 28.7 %collective-permute-start.11 = (bf16[128,1536]{1,0:T(8,128)(2,1)}, bf16[128,1536]{1,0:T(8,128)(2,1)}, u32[]{:S(2)}, u32[]{:S(2)}) collective-permute-start(bf16[128,1536]{1,0:T(8,128)(2,1)} %collective-permute-done.9), channel_id=1, source_target_pairs={{0,2},{2,4},{4,6},{6,8},{8,10},{10,12},{12,14},{14,16},{16,18},{18... | collective-permute-start | bytes 1179656 | tf_op jit(solution)/shard_map/ppermute | solution.py:16
  111.1 21.0 %collective-permute-start.12 = (bf16[128,1536]{1,0:T(8,128)(2,1)}, bf16[128,1536]{1,0:T(8,128)(2,1)}, u32[]{:S(2)}, u32[]{:S(2)}) collective-permute-start(bf16[128,1536]{1,0:T(8,128)(2,1)} %collective-permute-done.10), channel_id=1, source_target_pairs={{0,2},{2,4},{4,6},{6,8},{8,10},{10,12},{12,14},{14,16},{16,18},{18... | collective-permute-start | bytes 1179656 | tf_op jit(solution)/shard_map/ppermute | solution.py:16
  116.4 19.0 %collective-permute-start.13 = (bf16[128,1536]{1,0:T(8,128)(2,1)}, bf16[128,1536]{1,0:T(8,128)(2,1)}, u32[]{:S(2)}, u32[]{:S(2)}) collective-permute-start(bf16[128,1536]{1,0:T(8,128)(2,1)} %collective-permute-done.11), channel_id=1, source_target_pairs={{0,2},{2,4},{4,6},{6,8},{8,10},{10,12},{12,14},{14,16},{16,18},{18... | collective-permute-start | bytes 1179656 | tf_op jit(solution)/shard_map/ppermute | solution.py:16
  132.1 20.7 %collective-permute-start.14 = (bf16[128,1536]{1,0:T(8,128)(2,1)}, bf16[128,1536]{1,0:T(8,128)(2,1)}, u32[]{:S(2)}, u32[]{:S(2)}) collective-permute-start(bf16[128,1536]{1,0:T(8,128)(2,1)} %collective-permute-done.12), channel_id=1, source_target_pairs={{0,2},{2,4},{4,6},{6,8},{8,10},{10,12},{12,14},{14,16},{16,18},{18... | collective-permute-start | bytes 1179656 | tf_op jit(solution)/shard_map/ppermute | solution.py:16
  135.4 19.3 %collective-permute-start.15 = (bf16[128,1536]{1,0:T(8,128)(2,1)}, bf16[128,1536]{1,0:T(8,128)(2,1)}, u32[]{:S(2)}, u32[]{:S(2)}) collective-permute-start(bf16[128,1536]{1,0:T(8,128)(2,1)} %collective-permute-done.13), channel_id=1, source_target_pairs={{0,2},{2,4},{4,6},{6,8},{8,10},{10,12},{12,14},{14,16},{16,18},{18... | collective-permute-start | bytes 1179656 | tf_op jit(solution)/shard_map/ppermute | solution.py:16
  168.4 6.5 %copy-start.48 = (f32[16,128]{1,0:T(8,128)S(1)}, f32[16,128]{1,0:T(8,128)}, u32[]{:S(2)}) copy-start(f32[16,128]{1,0:T(8,128)} %get-tuple-element.75) | copy-start | bytes 24580
  168.4 6.5 %copy-start.51 = (f32[16,128]{1,0:T(8,128)S(1)}, f32[16,128]{1,0:T(8,128)}, u32[]{:S(2)}) copy-start(f32[16,128]{1,0:T(8,128)} %get-tuple-element.73) | copy-start | bytes 24580
  168.4 11.5 %copy-start.6 = (pred[128,2048]{1,0:T(8,128)(4,1)S(1)}, pred[128,2048]{1,0:T(8,128)(4,1)}, u32[]{:S(2)}) copy-start(pred[128,2048]{1,0:T(8,128)(4,1)} %compare_and_fusion) | copy-start | bytes 786436
  174.2 20.0 %copy-start.7 = (pred[128,2048]{1,0:T(8,128)(4,1)S(1)}, pred[128,2048]{1,0:T(8,128)(4,1)}, u32[]{:S(2)}) copy-start(pred[128,2048]{1,0:T(8,128)(4,1)} %compare_and_fusion) | copy-start | bytes 786436
  175.5 18.6 %copy-start.55 = (f32[16,128]{1,0:T(8,128)}, f32[16,128]{1,0:T(8,128)S(1)}, u32[]{:S(2)}) copy-start(f32[16,128]{1,0:T(8,128)S(1)} %get-tuple-element.44) | copy-start | bytes 24580
  194.2 10.6 %copy-start.8 = (f32[16,128,128]{1,2,0:T(8,128)S(1)}, f32[16,128,128]{1,2,0:T(8,128)}, u32[]{:S(2)}) copy-start(f32[16,128,128]{1,2,0:T(8,128)} %get-tuple-element.70) | copy-start | bytes 3145732
  194.2 10.6 %copy-start.29 = (pred[128,128]{0,1:T(8,128)(4,1)S(1)}, pred[128,128]{0,1:T(8,128)(4,1)}, u32[]{:S(2)}) copy-start(pred[128,128]{0,1:T(8,128)(4,1)} %get-tuple-element.58) | copy-start | bytes 49156
  194.2 10.6 %copy-start.56 = (f32[16,128]{1,0:T(8,128)S(1)}, f32[16,128]{1,0:T(8,128)}, u32[]{:S(2)}) copy-start(f32[16,128]{1,0:T(8,128)} %get-tuple-element.35) | copy-start | bytes 24580
  194.2 10.8 %copy-start.5 = (f32[16,128,128]{1,2,0:T(8,128)S(1)}, f32[16,128,128]{1,2,0:T(8,128)}, u32[]{:S(2)}) copy-start(f32[16,128,128]{1,2,0:T(8,128)} %get-tuple-element.72) | copy-start | bytes 3145732
  194.2 10.8 %copy-start.22 = (pred[128,128]{0,1:T(8,128)(4,1)S(1)}, pred[128,128]{0,1:T(8,128)(4,1)}, u32[]{:S(2)}) copy-start(pred[128,128]{0,1:T(8,128)(4,1)} %get-tuple-element.54) | copy-start | bytes 49156
  194.2 10.8 %copy-start.39 = (f32[16,128]{1,0:T(8,128)S(1)}, f32[16,128]{1,0:T(8,128)}, u32[]{:S(2)}) copy-start(f32[16,128]{1,0:T(8,128)} %get-tuple-element.36) | copy-start | bytes 24580
  194.2 11.0 %copy-start.4 = (f32[16,128,128]{1,2,0:T(8,128)S(1)}, f32[16,128,128]{1,2,0:T(8,128)}, u32[]{:S(2)}) copy-start(f32[16,128,128]{1,2,0:T(8,128)} %get-tuple-element.74) | copy-start | bytes 3145732
  194.3 11.0 %copy-start.23 = (pred[128,128]{0,1:T(8,128)(4,1)S(1)}, pred[128,128]{0,1:T(8,128)(4,1)}, u32[]{:S(2)}) copy-start(pred[128,128]{0,1:T(8,128)(4,1)} %get-tuple-element.56) | copy-start | bytes 49156
  194.3 11.0 %copy-start.40 = (f32[16,128]{1,0:T(8,128)S(1)}, f32[16,128]{1,0:T(8,128)}, u32[]{:S(2)}) copy-start(f32[16,128]{1,0:T(8,128)} %get-tuple-element.37) | copy-start | bytes 24580
  194.3 11.3 %copy-start.3 = (f32[16,128,128]{1,2,0:T(8,128)S(1)}, f32[16,128,128]{1,2,0:T(8,128)}, u32[]{:S(2)}) copy-start(f32[16,128,128]{1,2,0:T(8,128)} %get-tuple-element.76) | copy-start | bytes 3145732
  194.3 11.3 %copy-start.24 = (pred[128,128]{0,1:T(8,128)(4,1)S(1)}, pred[128,128]{0,1:T(8,128)(4,1)}, u32[]{:S(2)}) copy-start(pred[128,128]{0,1:T(8,128)(4,1)} %get-tuple-element.52) | copy-start | bytes 49156
  194.3 11.3 %copy-start.41 = (f32[16,128]{1,0:T(8,128)S(1)}, f32[16,128]{1,0:T(8,128)}, u32[]{:S(2)}) copy-start(f32[16,128]{1,0:T(8,128)} %get-tuple-element.38) | copy-start | bytes 24580
  194.3 11.5 %copy-start.2 = (f32[16,128,128]{1,2,0:T(8,128)S(1)}, f32[16,128,128]{1,2,0:T(8,128)}, u32[]{:S(2)}) copy-start(f32[16,128,128]{1,2,0:T(8,128)} %get-tuple-element.78) | copy-start | bytes 3145732
  194.3 11.5 %copy-start.42 = (f32[16,128]{1,0:T(8,128)S(1)}, f32[16,128]{1,0:T(8,128)}, u32[]{:S(2)}) copy-start(f32[16,128]{1,0:T(8,128)} %get-tuple-element.39) | copy-start | bytes 24580
  194.3 11.7 %copy-start.1 = (f32[16,128,128]{1,2,0:T(8,128)S(1)}, f32[16,128,128]{1,2,0:T(8,128)}, u32[]{:S(2)}) copy-start(f32[16,128,128]{1,2,0:T(8,128)} %get-tuple-element.80) | copy-start | bytes 3145732
  194.3 11.7 %copy-start.25 = (pred[128,128]{0,1:T(8,128)(4,1)S(1)}, pred[128,128]{0,1:T(8,128)(4,1)}, u32[]{:S(2)}) copy-start(pred[128,128]{0,1:T(8,128)(4,1)} %get-tuple-element.55) | copy-start | bytes 49156
  194.3 11.7 %copy-start.43 = (f32[16,128]{1,0:T(8,128)S(1)}, f32[16,128]{1,0:T(8,128)}, u32[]{:S(2)}) copy-start(f32[16,128]{1,0:T(8,128)} %get-tuple-element.40) | copy-start | bytes 24580
  194.4 11.9 %copy-start.26 = (pred[128,128]{0,1:T(8,128)(4,1)S(1)}, pred[128,128]{0,1:T(8,128)(4,1)}, u32[]{:S(2)}) copy-start(pred[128,128]{0,1:T(8,128)(4,1)} %get-tuple-element.53) | copy-start | bytes 49156
  194.4 11.9 %copy-start.44 = (f32[16,128]{1,0:T(8,128)S(1)}, f32[16,128]{1,0:T(8,128)}, u32[]{:S(2)}) copy-start(f32[16,128]{1,0:T(8,128)} %get-tuple-element.41) | copy-start | bytes 24580
  194.4 12.1 %copy-start.21 = (pred[128,128]{0,1:T(8,128)(4,1)S(1)}, pred[128,128]{0,1:T(8,128)(4,1)}, u32[]{:S(2)}) copy-start(pred[128,128]{0,1:T(8,128)(4,1)} %copy-done.20) | copy-start | bytes 49156
  194.4 12.1 %copy-start.45 = (f32[16,128]{1,0:T(8,128)S(1)}, f32[16,128]{1,0:T(8,128)}, u32[]{:S(2)}) copy-start(f32[16,128]{1,0:T(8,128)} %get-tuple-element.42) | copy-start | bytes 24580
  194.4 12.3 %copy-start.28 = (pred[128,128]{0,1:T(8,128)(4,1)S(1)}, pred[128,128]{0,1:T(8,128)(4,1)}, u32[]{:S(2)}) copy-start(pred[128,128]{0,1:T(8,128)(4,1)} %copy-done.27) | copy-start | bytes 49156
  194.4 12.3 %copy-start.46 = (f32[16,128]{1,0:T(8,128)S(1)}, f32[16,128]{1,0:T(8,128)}, u32[]{:S(2)}) copy-start(f32[16,128]{1,0:T(8,128)} %get-tuple-element.43) | copy-start | bytes 24580
  194.4 12.5 %copy-start.17 = (f32[16,128,8]{1,2,0:T(8,128)S(1)}, f32[16,128,8]{1,2,0:T(8,128)}, u32[]{:S(2)}) copy-start(f32[16,128,8]{1,2,0:T(8,128)} %get-tuple-element.90) | copy-start | bytes 196612
  194.4 13.5 %copy-start.31 = (f32[16,128]{1,0:T(8,128)S(1)}, f32[16,128]{1,0:T(8,128)}, u32[]{:S(2)}) copy-start(f32[16,128]{1,0:T(8,128)} %get-tuple-element.89) | copy-start | bytes 24580
  194.4 13.5 %copy-start.33 = (f32[16,128]{1,0:T(8,128)S(1)}, f32[16,128]{1,0:T(8,128)}, u32[]{:S(2)}) copy-start(f32[16,128]{1,0:T(8,128)} %get-tuple-element.83) | copy-start | bytes 24580
  194.4 13.5 %copy-start.35 = (f32[16,128]{1,0:T(8,128)S(1)}, f32[16,128]{1,0:T(8,128)}, u32[]{:S(2)}) copy-start(f32[16,128]{1,0:T(8,128)} %get-tuple-element.79) | copy-start | bytes 24580
  194.5 13.5 %copy-start.37 = (f32[16,128]{1,0:T(8,128)S(1)}, f32[16,128]{1,0:T(8,128)}, u32[]{:S(2)}) copy-start(f32[16,128]{1,0:T(8,128)} %copy-done.36) | copy-start | bytes 24580
  194.5 13.5 %copy-start.49 = (f32[16,128]{1,0:T(8,128)S(1)}, f32[16,128]{1,0:T(8,128)}, u32[]{:S(2)}) copy-start(f32[16,128]{1,0:T(8,128)} %get-tuple-element.75) | copy-start | bytes 24580
  194.5 14.3 %copy-start.38 = (bf16[8,16,96]{2,1,0:T(8,128)(2,1)S(1)}, bf16[8,16,96]{2,1,0:T(8,128)(2,1)}, u32[]{:S(2)}) copy-start(bf16[8,16,96]{2,1,0:T(8,128)(2,1)} %reshape.1640) | copy-start | bytes 73732
  194.5 15.4 %copy-start.9 = (bf16[128,1536]{0,1:T(8,128)(2,1)S(1)}, bf16[128,1536]{0,1:T(8,128)(2,1)}, u32[]{:S(2)}) copy-start(bf16[128,1536]{0,1:T(8,128)(2,1)} %copy.93) | copy-start | bytes 1179652
  194.5 15.7 %copy-start.10 = (bf16[128,1536]{0,1:T(8,128)(2,1)S(1)}, bf16[128,1536]{0,1:T(8,128)(2,1)}, u32[]{:S(2)}) copy-start(bf16[128,1536]{0,1:T(8,128)(2,1)} %copy.96) | copy-start | bytes 1179652
  204.8 6.7 %copy-start.13 = (bf16[128,1536]{0,1:T(8,128)(2,1)S(1)}, bf16[128,1536]{0,1:T(8,128)(2,1)}, u32[]{:S(2)}) copy-start(bf16[128,1536]{0,1:T(8,128)(2,1)} %copy.108) | copy-start | bytes 1179652
  204.8 7.0 %copy-start.16 = (bf16[128,1536]{0,1:T(8,128)(2,1)S(1)}, bf16[128,1536]{0,1:T(8,128)(2,1)}, u32[]{:S(2)}) copy-start(bf16[128,1536]{0,1:T(8,128)(2,1)} %copy.111) | copy-start | bytes 1179652
  204.8 7.4 %copy-start.15 = (bf16[128,1536]{0,1:T(8,128)(2,1)S(1)}, bf16[128,1536]{0,1:T(8,128)(2,1)}, u32[]{:S(2)}) copy-start(bf16[128,1536]{0,1:T(8,128)(2,1)} %copy.114) | copy-start | bytes 1179652
  205.3 7.2 %copy-start.18 = (bf16[128,1536]{0,1:T(8,128)(2,1)S(1)}, bf16[128,1536]{0,1:T(8,128)(2,1)}, u32[]{:S(2)}) copy-start(bf16[128,1536]{0,1:T(8,128)(2,1)} %copy.117) | copy-start | bytes 1179652
  (16 other events, 84.1 us)
Sparse Core Ops, SparseCore 0:
  9.6 76.9 all-gather.2
  88.9 72.0 all-gather.4
  215.7 28.4 reduce-scatter.1
where the time goes:
time: 255 us; the launch traced here: 253 us
  starting transfers between devices  88 us (35%)
  local copies, waits for them, and re-layouts  59.2 us (23%)
  matrix products  45.1 us (18%)
  waiting for transfers between devices  30.1 us (12%)
  other arithmetic  16 us (6%)
  between operations  14.3 us (6%)
    ppermute x16, starting transfers between devices, from_behind(): return lax.ppermute(array, axis, pairs)  87.9 us
    dot_general x11, matrix products, absorb(): jnp.einsum('shd,khd->hsk', q_three, k_three, preferred_element_type=jnp.f...  28.8 us
    reduce_scatter x1, waiting for transfers between devices, shards(): lax.psum_scatter(jnp.einsum('cd,sc->ds', w_out, attn, preferred_element_t...  28.6 us
    ppermute x16, local copies, waits for them, and re-layouts, from_behind(): return lax.ppermute(array, axis, pairs)  28.2 us
    dot_general x11, matrix products, absorb(): jnp.einsum('hsk,khd->hsd', prob.astype(jnp.bfloat16), v_three, preferred_...  14.1 us
    unnamed x125, local copies, waits for them, and re-layouts  9.44 us
    all_gather x1, local copies, waits for them, and re-layouts, shards(): lax.all_gather(cache_k, 'seq', axis=0, tiled=True)  8.67 us
    all_gather x1, local copies, waits for them, and re-layouts, shards(): lax.all_gather(cache_v, 'seq', axis=0, tiled=True)  8.66 us
  transfers between devices with their start and end apart: 19, of which 1 were waited for; matrix products, arithmetic and copies ran while one was open for 33% of the time, Pallas kernels for 0%

commit v1 on v0

--- a/solution.py
+++ b/solution.py
@@ -1,13 +1,21 @@
+import functools
 import math
 
 import jax
 import jax.numpy as jnp
 from jax import lax
+from jax.experimental import pallas as pl
+from jax.experimental.pallas import tpu as pltpu
 from jax.sharding import PartitionSpec as P
 
 HD = 96
 W = 1024
 SINKS = 4
+
+
+def starts_of(lengths):
+    place = jnp.arange(lengths.shape[0], dtype=jnp.int32)
+    return jnp.sum(jnp.where(place[None, :] < place[:, None], lengths[None, :], 0), axis=1)
 
 
 def from_behind(array, axis, by):
@@ -27,14 +35,14 @@
     return (request, offset, group)
 
 
-def shards(
+def gathered(
     queries, keys, values, cache_k, cache_v, sink_k, sink_v, suffix_lengths, request_group, w_out
 ):
     rows, width = queries.shape
     heads = width // HD
     scale = 1.0 / math.sqrt(HD)
     device = lax.axis_index("seq")
-    starts = jnp.cumsum(suffix_lengths) - suffix_lengths
+    starts = starts_of(suffix_lengths)
     index = device * rows + jnp.arange(rows, dtype=jnp.int32)
     req_q, off_q, grp_q = describe(index, starts, suffix_lengths, request_group)
     q_three = queries.reshape(rows, heads, HD)
@@ -104,6 +112,263 @@
     )
 
 
+TILE = 256
+
+
+def greet(me, n):
+    barrier = pltpu.get_barrier_semaphore()
+
+    def one(o, carry):
+        pl.semaphore_signal(
+            barrier,
+            inc=1,
+            device_id={"seq": lax.rem(me + o, n)},
+            device_id_type=pl.DeviceIdType.MESH,
+        )
+        return carry
+
+    lax.fori_loop(1, n, one, 0)
+    pl.semaphore_wait(barrier, n - 1)
+
+
+def exchange(me, n, source, landing, send_sem, recv_sem, local_sem):
+    def copy_to(o):
+        to = lax.rem(me + o, n)
+        return pltpu.make_async_remote_copy(
+            src_ref=source.at[to],
+            dst_ref=landing.at[me],
+            send_sem=send_sem.at[o],
+            recv_sem=recv_sem.at[o],
+            device_id={"seq": to},
+            device_id_type=pl.DeviceIdType.MESH,
+        )
+
+    def start(o, carry):
+        copy_to(o).start()
+        return carry
+
+    def finish(o, carry):
+        copy_to(o).wait()
+        return carry
+
+    own = pltpu.make_async_copy(source.at[me], landing.at[me], local_sem)
+    lax.fori_loop(1, n, start, 0)
+    own.start()
+    lax.fori_loop(1, n, finish, 0)
+    own.wait()
+
+
+def to_heads_kernel(n, q, k, v, ck, cv, out, stage, send_sem, recv_sem, local_sem):
+    me = lax.axis_index("seq")
+    rows = q.shape[0]
+    for a, ref in enumerate((q, k, v, ck, cv)):
+        for g in range(n // 4):
+            turned = ref[:, g * 4 * HD : (g + 1) * 4 * HD].T
+            for i in range(4):
+                stage[4 * g + i, a] = turned[i * HD : (i + 1) * HD]
+    greet(me, n)
+    exchange(me, n, stage, out, send_sem, recv_sem, local_sem)
+
+
+def to_heads(n, *arrays):
+    rows = arrays[0].shape[0]
+    shape = (n, len(arrays), HD, rows)
+    return pl.pallas_call(
+        functools.partial(to_heads_kernel, n),
+        out_shape=jax.ShapeDtypeStruct(shape, jnp.bfloat16),
+        in_specs=[pl.BlockSpec(memory_space=pltpu.VMEM)] * len(arrays),
+        out_specs=pl.BlockSpec(memory_space=pl.ANY),
+        scratch_shapes=[
+            pltpu.VMEM(shape, jnp.bfloat16),
+            pltpu.SemaphoreType.DMA((n,)),
+            pltpu.SemaphoreType.DMA((n,)),
+            pltpu.SemaphoreType.DMA,
+        ],
+        compiler_params=pltpu.CompilerParams(
+            collective_id=0, has_side_effects=True, vmem_limit_bytes=32 << 20
+        ),
+        name="to_heads",
+    )(*arrays)
+
+
+def attend_kernel(
+    tokens, slots, lengths, groups, info, x, sk, sv, out, q_t, v_t, cv_t, k_n, ck_n
+):
+    n, _, _, rows = x.shape
+    count = lengths.shape[0]
+    own = slots // W
+    factor = math.log2(math.e) / math.sqrt(HD)
+    for b in range(n):
+        at = pl.ds(b * rows, rows)
+        q_t[:, at] = x[b, 0]
+        k_n[at, :] = x[b, 1].T
+        v_t[:, at] = x[b, 2]
+        ck_n[at, :] = x[b, 3].T
+        cv_t[:, at] = x[b, 4]
+    column = lax.broadcasted_iota(jnp.int32, (TILE, 1), 0)
+    sink_column = lax.broadcasted_iota(jnp.int32, (sk.shape[0], 1), 0) // SINKS
+
+    def tile(i, carry):
+        first = i * TILE
+        last = first + TILE
+        begin = jnp.int32(0)
+        earliest = first
+        lowest = [jnp.int32(W) for _ in range(own)]
+        for r in range(count):
+            end = begin + lengths[r]
+            low = jnp.maximum(first, begin)
+            touches = low < jnp.minimum(last, end)
+            earliest = jnp.where(touches, jnp.minimum(earliest, begin), earliest)
+            for g in range(own):
+                lowest[g] = jnp.where(
+                    touches & (groups[r] == g), jnp.minimum(lowest[g], low - begin), lowest[g]
+                )
+            begin = end
+        here = pl.ds(pl.multiple_of(first, TILE), TILE)
+        q_tile = q_t[:, here]
+        start_q = info[0:1, here]
+        group_q = info[1:2, here]
+        index_q = first + lax.broadcasted_iota(jnp.int32, (1, TILE), 1)
+        offset_q = index_q - start_q
+
+        score = jnp.dot(sk[...], q_tile, preferred_element_type=jnp.float32)
+        score = jnp.where(sink_column == group_q, score, jnp.float32(-1e30))
+        top = jnp.max(score, axis=0, keepdims=True)
+        prob = jnp.exp2((score - top) * factor)
+        den = jnp.sum(prob, axis=0, keepdims=True)
+        acc = jnp.dot(sv[...], prob.astype(jnp.bfloat16), preferred_element_type=jnp.float32)
+
+        def absorb(state, key_rows, value_columns, mask):
+            top, den, acc = state
+            score = jnp.dot(key_rows, q_tile, preferred_element_type=jnp.float32)
+            score = jnp.where(mask, score, jnp.float32(-1e30))
+            new_top = jnp.maximum(top, jnp.max(score, axis=0, keepdims=True))
+            shrink = jnp.exp2((top - new_top) * factor)
+            prob = jnp.exp2((score - new_top) * factor)
+            den = den * shrink + jnp.sum(prob, axis=0, keepdims=True)
+            acc = acc * shrink + jnp.dot(
+                value_columns, prob.astype(jnp.bfloat16), preferred_element_type=jnp.float32
+            )
+            return new_top, den, acc
+
+        state = (top, den, acc)
+        for g in range(own):
+            limit = jnp.where(group_q == g, offset_q, jnp.int32(W))
+
+            def cached(c, state):
+                at = pl.ds(pl.multiple_of(g * W + c * TILE, TILE), TILE)
+                mask = c * TILE + column > limit
+                return absorb(state, ck_n[at, :], cv_t[:, at], mask)
+
+            state = lax.fori_loop((lowest[g] + 1) // TILE, W // TILE, cached, state)
+
+        def suffix(c, state):
+            at = pl.ds(pl.multiple_of(c * TILE, TILE), TILE)
+            index_k = c * TILE + column
+            return absorb(
+                state, k_n[at, :], v_t[:, at], (index_k >= start_q) & (index_k <= index_q)
+            )
+
+        top, den, acc = lax.fori_loop(earliest // TILE, i + 1, suffix, state)
+        result = (acc / den).astype(jnp.bfloat16)
+        for part in range(TILE // rows):
+            out[i * (TILE // rows) + part] = result[:, part * rows : (part + 1) * rows]
+        return carry
+
+    lax.fori_loop(0, tokens // TILE, tile, 0)
+
+
+def attend(x, sk, sv, lengths, groups, info):
+    n, _, _, rows = x.shape
+    tokens = n * rows
+    vmem = pl.BlockSpec(memory_space=pltpu.VMEM)
+    smem = pl.BlockSpec(memory_space=pltpu.SMEM)
+    return pl.pallas_call(
+        functools.partial(attend_kernel, tokens, tokens),
+        out_shape=jax.ShapeDtypeStruct((n, HD, rows), jnp.bfloat16),
+        in_specs=[smem, smem, vmem, vmem, vmem, vmem],
+        out_specs=vmem,
+        scratch_shapes=[
+            pltpu.VMEM((HD, tokens), jnp.bfloat16),
+            pltpu.VMEM((HD, tokens), jnp.bfloat16),
+            pltpu.VMEM((HD, tokens), jnp.bfloat16),
+            pltpu.VMEM((tokens, HD), jnp.bfloat16),
+            pltpu.VMEM((tokens, HD), jnp.bfloat16),
+        ],
+        compiler_params=pltpu.CompilerParams(vmem_limit_bytes=32 << 20),
+        name="attend",
+    )(lengths, groups, info, x, sk, sv)
+
+
+def to_tokens_kernel(n, x, out, send_sem, recv_sem, local_sem):
+    me = lax.axis_index("seq")
+    greet(me, n)
+    exchange(me, n, x, out, send_sem, recv_sem, local_sem)
+
+
+def to_tokens(x):
+    n = x.shape[0]
+    return pl.pallas_call(
+        functools.partial(to_tokens_kernel, n),
+        out_shape=jax.ShapeDtypeStruct(x.shape, x.dtype),
+        in_specs=[pl.BlockSpec(memory_space=pltpu.VMEM)],
+        out_specs=pl.BlockSpec(memory_space=pl.ANY),
+        scratch_shapes=[
+            pltpu.SemaphoreType.DMA((n,)),
+            pltpu.SemaphoreType.DMA((n,)),
+            pltpu.SemaphoreType.DMA,
+        ],
+        compiler_params=pltpu.CompilerParams(collective_id=1, has_side_effects=True),
+        name="to_tokens",
+    )(x)
+
+
+def by_heads(
+    queries, keys, values, cache_k, cache_v, sink_k, sink_v, suffix_lengths, request_group, w_out
+):
+    n = lax.axis_size("seq")
+    rows, width = queries.shape
+    starts = starts_of(suffix_lengths)
+    index = jnp.arange(n * rows, dtype=jnp.int32)
+    inside = (starts[:, None] <= index[None, :]) & (
+        index[None, :] < (starts + suffix_lengths)[:, None]
+    )
+    info = jnp.stack(
+        [
+            jnp.sum(jnp.where(inside, starts[:, None], 0), axis=0),
+            jnp.sum(jnp.where(inside, request_group[:, None], 0), axis=0),
+        ]
+    )
+    me = lax.axis_index("seq")
+    sk = lax.dynamic_slice_in_dim(sink_k, me * HD, HD, 1)
+    sv = lax.dynamic_slice_in_dim(sink_v, me * HD, HD, 1).T
+    x = to_heads(n, queries, keys, values, cache_k, cache_v)
+    attn = attend(x, sk, sv, suffix_lengths, request_group, info)
+    attn = to_tokens(attn).reshape(width, rows)
+    return lax.psum_scatter(
+        jnp.einsum("cd,cs->ds", w_out, attn, preferred_element_type=jnp.float32).astype(
+            jnp.bfloat16
+        ),
+        "head",
+        scatter_dimension=0,
+        tiled=True,
+    )
+
+
+def shards(queries, keys, values, cache_k, *rest):
+    n = lax.axis_size("seq")
+    rows, width = queries.shape
+    fits = (
+        n == width // HD
+        and n % 4 == 0
+        and rows % 128 == 0
+        and TILE % rows == 0
+        and cache_k.shape[0] == rows
+        and (n * rows) % W == 0
+    )
+    return (by_heads if fits else gathered)(queries, keys, values, cache_k, *rest)
+
+
 def solution(mesh):
     placed = (
         P("seq", "head"),

time: 255 us -> 141 us (0.55)
  starting transfers between devices: 88 us -> 0.01 us
  Pallas kernels: 0 us -> 87.6 us
  local copies, waits for them, and re-layouts: 59.2 us -> 9.82 us
  matrix products: 45.1 us -> 6.13 us
  other arithmetic: 16 us -> 2.23 us
  waiting for transfers between devices: 30.1 us -> 20.5 us
    ppermute x16 -> x0, starting transfers between devices: 87.9 us -> none  [from_behind(): return lax.ppermute(array, axis, pairs)]
    pallas_call x0 -> x3, Pallas kernels: none -> 87.6 us  [the longest x1 39.1 us: to_heads(): pl.pallas_call(functools.partial(to_heads_kernel, n), out_shape=jax.Shape...]
    dot_general x23 -> x1, matrix products: 45.1 us -> 6.13 us  [by_heads(): jnp.einsum('cd,cs->ds', w_out, attn, preferred_element_type=jnp.float32)]
    ppermute x16 -> x0, local copies, waits for them, and re-layouts: 28.2 us -> none  [from_behind(): return lax.ppermute(array, axis, pairs)]
    all_gather x2 -> x0, local copies, waits for them, and re-layouts: 17.3 us -> none  [the longest x1 8.67 us: shards(): lax.all_gather(cache_k, 'seq', axis=0, tiled=True)]
    reduce_scatter x1, waiting for transfers between devices: 28.6 us -> 20.5 us  [by_heads(): lax.psum_scatter(jnp.einsum('cd,cs->ds', w_out, attn, preferred_element_t...]
    reduce_sum x16 -> x2, other arithmetic: 9.16 us -> 1.55 us  [the longest x1 0.78 us: by_heads(): jnp.sum(jnp.where(inside, starts[:, None], 0), axis=0)]
    and x4 -> x0, other arithmetic: 2.99 us -> none  [the longest x2 1.93 us: suffix_mask(): (req_k[None, :] == req_q[:, None]) & (near[None, :] <= index[:, None])]
  transfers between devices with their start and end apart: 19 -> 1, of which waited for: 1 -> 1; matrix products, arithmetic and copies ran while one was open for 33% -> 0% of each run, Pallas kernels for 0% -> 0%
where the time goes in v1:
time: 141 us; the launch traced here: 140 us
  Pallas kernels  87.6 us (62%)
  waiting for transfers between devices  20.5 us (15%)
  between operations  13.5 us (10%)
  local copies, waits for them, and re-layouts  9.82 us (7%)
  matrix products  6.13 us (4%)
  other arithmetic  2.23 us (2%)
    pallas_call x1, Pallas kernels, to_heads(): pl.pallas_call(functools.partial(to_heads_kernel, n), out_shape=jax.Shape...  39.1 us
    pallas_call x1, Pallas kernels, attend(): pl.pallas_call(functools.partial(attend_kernel, tokens, tokens), out_shap...  26.1 us
    pallas_call x1, Pallas kernels, to_tokens(): pl.pallas_call(functools.partial(to_tokens_kernel, n), out_shape=jax.Shap...  22.5 us
    reduce_scatter x1, waiting for transfers between devices, by_heads(): lax.psum_scatter(jnp.einsum('cd,cs->ds', w_out, attn, preferred_element_t...  20.5 us
    unnamed x17, local copies, waits for them, and re-layouts  7.13 us
    dot_general x1, matrix products, by_heads(): jnp.einsum('cd,cs->ds', w_out, attn, preferred_element_type=jnp.float32)  6.13 us
  transfers between devices with their start and end apart: 1, of which 1 were waited for; matrix products, arithmetic and copies ran while one was open for 0% of the time, Pallas kernels for 0%

profile of v1, /device:TPU:0, one launch (start us, length us, event | category | flops | bytes accessed | tf_op | source)
XLA Modules:
  0.0 139.8 jit_solution(9606614561953878689)
XLA Ops:
  6.5 0.0 reduce-scatter.2.cloned.1.call-start
  6.5 0.8 select_reduce_fusion.2
  7.3 0.7 add.9
  8.0 0.8 constant_dynamic-slice_fusion
  8.7 0.1 copy.15
  8.9 0.8 select_reduce_fusion.1
  9.7 0.0 copy-start.1
  9.7 1.0 copy-done.1
  10.7 0.0 copy-start.2
  10.7 1.0 copy-done.2
  11.7 0.0 copy-start.3
  11.7 1.0 copy-done.3
  12.7 0.0 copy-start.4
  12.7 1.0 copy-done.4
  13.7 0.0 copy-start.5
  13.7 1.0 copy-done.5
  14.7 39.1 %to_heads.1.x = bf16[16,5,96,128]{3,2,1,0:T(8,128)(2,1)S(1)} custom-call(bf16[128,1536]{1,0:T(8,128)(2,1)S(1)} %copy-done.1, bf16[128,1536]{1,0:T(8,128)(2,1)S(1)} %copy-done.2, bf16[128,1536]{1,0:T(8,128)(2,1)S(1)} %copy-done.3, bf16[128,1536]{1,0:T(8,128)(2,1)S(1)} %copy-done.4, bf16[128,1536]{1,0:T(8,128)(2,1)S(1)} %copy-done.5), custom_call_target="tpu_custom_call" | custom-call | tf_op jit(solution)/shard_map/to_heads/pallas_call | solution.py:176
  53.7 0.0 copy-start.6
  53.7 0.6 copy-done.6
  54.4 0.0 copy-start.7
  54.4 0.7 copy-done.7
  55.0 26.1 %attend.1.x = bf16[16,96,128]{2,1,0:T(8,128)(2,1)S(1)} custom-call(s32[4]{0:T(128)S(1)} %copy-done.7, s32[4]{0:T(128)S(1)} %copy-done.6, s32[2,2048]{1,0:T(2,128)S(1)} %pad_add_fusion.info, bf16[16,5,96,128]{3,2,1,0:T(8,128)(2,1)S(1)} %to_heads.1.x, bf16[8,96]{1,0:T(8,128)(2,1)S(1)} %get-tuple-element.7.sk, bf16[96,8]{1,0:T(8,128)(2,1)S(1)} %bitcast.8), custom_call_target="tpu_custom_call" | custom-call | tf_op jit(solution)/shard_map/attend/pallas_call | solution.py:286
  81.2 0.0 copy-start
  81.2 0.7 copy-done
  81.9 22.5 %to_tokens.1 = bf16[16,96,128]{2,1,0:T(8,128)(2,1)} custom-call(bf16[16,96,128]{2,1,0:T(8,128)(2,1)} %copy-done), custom_call_target="tpu_custom_call" | custom-call | tf_op jit(solution)/shard_map/to_tokens/pallas_call | solution.py:311
  104.4 6.1 %fusion = bf16[3072,128]{0,1:T(8,128)(2,1)} fusion(bf16[1536,128]{1,0:T(8,128)(2,1)} %bitcast.9, bf16[1536,3072]{1,0:T(8,128)(2,1)} %param.19), kind=kOutput, calls=%fused_computation.1 | convolution fusion | flops 1208352768 | bytes 10616832 | tf_op jit(solution)/shard_map/cd,cs->ds/dot_general | solution.py:349
  110.5 0.0 reduce-scatter.2.cloned.1.call-update
  110.5 20.5 %reduce-scatter.2.cloned.1.call-done = bf16[1536,128]{0,1:T(8,128)(2,1)} async-done(((bf16[3072,128]{0,1:T(8,128)(2,1)}), bf16[1536,128]{0,1:T(8,128)(2,1)}) %reduce-scatter.2.cloned.1.call-update) | async-done | bytes 393232 | tf_op jit(solution)/shard_map/reduce_scatter | solution.py:348
  131.0 1.9 %copy.14 = bf16[1536,128]{1,0:T(8,128)(2,1)} copy(bf16[1536,128]{0,1:T(8,128)(2,1)} %reduce-scatter.2.cloned.1.call-done) | data formatting | bytes 786432 | tf_op jit(solution)/shard_map/reduce_scatter | solution.py:348
  (1 shorter events, 0.0 us)
Async XLA Ops:
  6.5 124.5 %reduce-scatter.2.cloned.1.call-start = ((), (), s32[]{:S(2)}) async-start(), calls=%async_computation.1 | async-start | bytes 1179648 | tf_op jit(solution)/shard_map/reduce_scatter | solution.py:348
  9.7 1.0 copy-start.1
  10.7 1.0 copy-start.2
  11.7 1.0 copy-start.3
  12.7 1.0 copy-start.4
  13.7 1.0 copy-start.5
  53.7 0.7 copy-start.6
  54.4 0.7 copy-start.7
  81.2 0.7 copy-start
Sparse Core Ops, SparseCore 0:
  110.7 20.3 reduce-scatter.1

commit v2 on v1

--- a/solution.py
+++ b/solution.py
@@ -115,7 +115,7 @@
 TILE = 256
 
 
-def greet(me, n):
+def greet(me, n, extra=()):
     barrier = pltpu.get_barrier_semaphore()
 
     def one(o, carry):
@@ -128,7 +128,14 @@
         return carry
 
     lax.fori_loop(1, n, one, 0)
-    pl.semaphore_wait(barrier, n - 1)
+    for other in extra:
+        pl.semaphore_signal(
+            barrier, inc=1, device_id={"head": other}, device_id_type=pl.DeviceIdType.MESH
+        )
+
+
+def greeted(count):
+    pl.semaphore_wait(pltpu.get_barrier_semaphore(), count)
 
 
 def exchange(me, n, source, landing, send_sem, recv_sem, local_sem):
@@ -143,77 +150,107 @@
             device_id_type=pl.DeviceIdType.MESH,
         )
 
-    def start(o, carry):
+    def one_start(o, carry):
         copy_to(o).start()
         return carry
 
-    def finish(o, carry):
+    def one_end(o, carry):
         copy_to(o).wait()
         return carry
 
     own = pltpu.make_async_copy(source.at[me], landing.at[me], local_sem)
-    lax.fori_loop(1, n, start, 0)
-    own.start()
-    lax.fori_loop(1, n, finish, 0)
-    own.wait()
-
-
-def to_heads_kernel(n, q, k, v, ck, cv, out, stage, send_sem, recv_sem, local_sem):
+
+    def start():
+        lax.fori_loop(1, n, one_start, 0)
+        own.start()
+
+    def end():
+        lax.fori_loop(1, n, one_end, 0)
+        own.wait()
+
+    return start, end
+
+
+def to_heads_kernel(n, *refs):
+    five, (first, second), refs = refs[:5], refs[5:7], refs[7:]
+    raw, stage_one, stage_two, load_sem, send_sem, recv_sem, local_sem = refs
     me = lax.axis_index("seq")
-    rows = q.shape[0]
-    for a, ref in enumerate((q, k, v, ck, cv)):
-        for g in range(n // 4):
-            turned = ref[:, g * 4 * HD : (g + 1) * 4 * HD].T
-            for i in range(4):
-                stage[4 * g + i, a] = turned[i * HD : (i + 1) * HD]
+    loads = [pltpu.make_async_copy(five[a], raw.at[a], load_sem.at[a]) for a in range(5)]
+    for load in loads:
+        load.start()
     greet(me, n)
-    exchange(me, n, stage, out, send_sem, recv_sem, local_sem)
+    ends = []
+    for which, (stage, landing, arrays) in enumerate(
+        ((stage_one, first, (0, 1, 2)), (stage_two, second, (3, 4)))
+    ):
+        for place, a in enumerate(arrays):
+            loads[a].wait()
+            for g in range(n // 4):
+                turned = raw[a, :, g * 4 * HD : (g + 1) * 4 * HD].T
+                for i in range(4):
+                    stage[4 * g + i, place] = turned[i * HD : (i + 1) * HD]
+        if which == 0:
+            greeted(n - 1)
+        start, end = exchange(
+            me, n, stage, landing, send_sem.at[which], recv_sem.at[which], local_sem.at[which]
+        )
+        start()
+        ends.append(end)
+    for end in ends:
+        end()
 
 
 def to_heads(n, *arrays):
-    rows = arrays[0].shape[0]
-    shape = (n, len(arrays), HD, rows)
+    rows, width = arrays[0].shape
+    shapes = [(n, 3, HD, rows), (n, 2, HD, rows)]
+    anywhere = pl.BlockSpec(memory_space=pl.ANY)
     return pl.pallas_call(
         functools.partial(to_heads_kernel, n),
-        out_shape=jax.ShapeDtypeStruct(shape, jnp.bfloat16),
-        in_specs=[pl.BlockSpec(memory_space=pltpu.VMEM)] * len(arrays),
-        out_specs=pl.BlockSpec(memory_space=pl.ANY),
+        out_shape=[jax.ShapeDtypeStruct(shape, jnp.bfloat16) for shape in shapes],
+        in_specs=[anywhere] * 5,
+        out_specs=[anywhere] * 2,
         scratch_shapes=[
-            pltpu.VMEM(shape, jnp.bfloat16),
-            pltpu.SemaphoreType.DMA((n,)),
-            pltpu.SemaphoreType.DMA((n,)),
-            pltpu.SemaphoreType.DMA,
+            pltpu.VMEM((5, rows, width), jnp.bfloat16),
+            pltpu.VMEM(shapes[0], jnp.bfloat16),
+            pltpu.VMEM(shapes[1], jnp.bfloat16),
+            pltpu.SemaphoreType.DMA((5,)),
+            pltpu.SemaphoreType.DMA((2, n)),
+            pltpu.SemaphoreType.DMA((2, n)),
+            pltpu.SemaphoreType.DMA((2,)),
         ],
         compiler_params=pltpu.CompilerParams(
-            collective_id=0, has_side_effects=True, vmem_limit_bytes=32 << 20
+            collective_id=0, has_side_effects=True, vmem_limit_bytes=48 << 20
         ),
         name="to_heads",
     )(*arrays)
 
 
-def attend_kernel(
-    tokens, slots, lengths, groups, info, x, sk, sv, out, q_t, v_t, cv_t, k_n, ck_n
-):
-    n, _, _, rows = x.shape
+def attend_kernel(tokens, slots, lengths, groups, one, two, sk, sv, out, q_t, k_n, v_t):
+    n, _, _, rows = one.shape
     count = lengths.shape[0]
     own = slots // W
     factor = math.log2(math.e) / math.sqrt(HD)
     for b in range(n):
         at = pl.ds(b * rows, rows)
-        q_t[:, at] = x[b, 0]
-        k_n[at, :] = x[b, 1].T
-        v_t[:, at] = x[b, 2]
-        ck_n[at, :] = x[b, 3].T
-        cv_t[:, at] = x[b, 4]
+        later = pl.ds(slots + b * rows, rows)
+        q_t[:, at] = one[b, 0]
+        k_n[later, :] = one[b, 1].T
+        v_t[:, later] = one[b, 2]
+        k_n[at, :] = two[b, 0].T
+        v_t[:, at] = two[b, 1]
     column = lax.broadcasted_iota(jnp.int32, (TILE, 1), 0)
     sink_column = lax.broadcasted_iota(jnp.int32, (sk.shape[0], 1), 0) // SINKS
+    far = jnp.int32(1 << 30)
 
     def tile(i, carry):
         first = i * TILE
         last = first + TILE
+        index_q = first + lax.broadcasted_iota(jnp.int32, (1, TILE), 1)
         begin = jnp.int32(0)
         earliest = first
         lowest = [jnp.int32(W) for _ in range(own)]
+        start_q = jnp.zeros((1, TILE), jnp.int32)
+        group_q = jnp.zeros((1, TILE), jnp.int32)
         for r in range(count):
             end = begin + lengths[r]
             low = jnp.maximum(first, begin)
@@ -223,13 +260,44 @@
                 lowest[g] = jnp.where(
                     touches & (groups[r] == g), jnp.minimum(lowest[g], low - begin), lowest[g]
                 )
+            inside = index_q >= begin
+            start_q = jnp.where(inside, begin, start_q)
+            group_q = jnp.where(inside, groups[r], group_q)
             begin = end
-        here = pl.ds(pl.multiple_of(first, TILE), TILE)
-        q_tile = q_t[:, here]
-        start_q = info[0:1, here]
-        group_q = info[1:2, here]
-        index_q = first + lax.broadcasted_iota(jnp.int32, (1, TILE), 1)
         offset_q = index_q - start_q
+        sections = []
+        for g in range(own):
+            chunk = (lowest[g] + 1) // TILE
+            limit = g * W + jnp.where(group_q == g, offset_q, jnp.int32(W))
+            sections.append(
+                (g * (W // TILE) + chunk, W // TILE - chunk, limit, jnp.zeros_like(limit) + far)
+            )
+        chunk = earliest // TILE
+        sections.append(
+            (slots // TILE + chunk, i + 1 - chunk, slots + start_q - 1, slots + index_q)
+        )
+        total = sum(section[1] for section in sections)
+
+        def find(t):
+            chunk, low, high = sections[0][0] + t, sections[0][2], sections[0][3]
+            before = sections[0][1]
+            for begins, number, lower, upper in sections[1:]:
+                here = t >= before
+                chunk = jnp.where(here, begins + t - before, chunk)
+                low = jnp.where(here, lower, low)
+                high = jnp.where(here, upper, high)
+                before = before + number
+            return pl.multiple_of(chunk * TILE, TILE), low, high
+
+        q_tile = q_t[:, pl.ds(pl.multiple_of(first, TILE), TILE)]
+
+        def scores(t):
+            at, _, _ = find(t)
+            return jnp.dot(k_n[pl.ds(at, TILE), :], q_tile, preferred_element_type=jnp.float32)
+
+        def weigh(t, prob):
+            at, _, _ = find(t)
+            return jnp.dot(v_t[:, pl.ds(at, TILE)], prob, preferred_element_type=jnp.float32)
 
         score = jnp.dot(sk[...], q_tile, preferred_element_type=jnp.float32)
         score = jnp.where(sink_column == group_q, score, jnp.float32(-1e30))
@@ -238,38 +306,22 @@
         den = jnp.sum(prob, axis=0, keepdims=True)
         acc = jnp.dot(sv[...], prob.astype(jnp.bfloat16), preferred_element_type=jnp.float32)
 
-        def absorb(state, key_rows, value_columns, mask):
-            top, den, acc = state
-            score = jnp.dot(key_rows, q_tile, preferred_element_type=jnp.float32)
-            score = jnp.where(mask, score, jnp.float32(-1e30))
+        def step(t, state):
+            top, den, acc, score, prob = state
+            following = scores(jnp.minimum(t + 1, total - 1))
+            acc = acc + weigh(jnp.maximum(t - 1, 0), prob)
+            at, low, high = find(t)
+            index_k = at + column
+            score = jnp.where((index_k > low) & (index_k <= high), score, jnp.float32(-1e30))
             new_top = jnp.maximum(top, jnp.max(score, axis=0, keepdims=True))
             shrink = jnp.exp2((top - new_top) * factor)
             prob = jnp.exp2((score - new_top) * factor)
             den = den * shrink + jnp.sum(prob, axis=0, keepdims=True)
-            acc = acc * shrink + jnp.dot(
-                value_columns, prob.astype(jnp.bfloat16), preferred_element_type=jnp.float32
-            )
-            return new_top, den, acc
-
-        state = (top, den, acc)
-        for g in range(own):
-            limit = jnp.where(group_q == g, offset_q, jnp.int32(W))
-
-            def cached(c, state):
-                at = pl.ds(pl.multiple_of(g * W + c * TILE, TILE), TILE)
-                mask = c * TILE + column > limit
-                return absorb(state, ck_n[at, :], cv_t[:, at], mask)
-
-            state = lax.fori_loop((lowest[g] + 1) // TILE, W // TILE, cached, state)
-
-        def suffix(c, state):
-            at = pl.ds(pl.multiple_of(c * TILE, TILE), TILE)
-            index_k = c * TILE + column
-            return absorb(
-                state, k_n[at, :], v_t[:, at], (index_k >= start_q) & (index_k <= index_q)
-            )
-
-        top, den, acc = lax.fori_loop(earliest // TILE, i + 1, suffix, state)
+            return new_top, den, acc * shrink, following, prob.astype(jnp.bfloat16)
+
+        state = (top, den, acc, scores(0), jnp.zeros((TILE, TILE), jnp.bfloat16))
+        top, den, acc, score, prob = lax.fori_loop(0, total, step, state)
+        acc = acc + weigh(total - 1, prob)
         result = (acc / den).astype(jnp.bfloat16)
         for part in range(TILE // rows):
             out[i * (TILE // rows) + part] = result[:, part * rows : (part + 1) * rows]
@@ -278,81 +330,122 @@
     lax.fori_loop(0, tokens // TILE, tile, 0)
 
 
-def attend(x, sk, sv, lengths, groups, info):
-    n, _, _, rows = x.shape
-    tokens = n * rows
+def attend(one, two, sk, sv, lengths, groups):
+    n, _, _, rows = one.shape
+    tokens = slots = n * rows
     vmem = pl.BlockSpec(memory_space=pltpu.VMEM)
     smem = pl.BlockSpec(memory_space=pltpu.SMEM)
     return pl.pallas_call(
-        functools.partial(attend_kernel, tokens, tokens),
+        functools.partial(attend_kernel, tokens, slots),
         out_shape=jax.ShapeDtypeStruct((n, HD, rows), jnp.bfloat16),
         in_specs=[smem, smem, vmem, vmem, vmem, vmem],
         out_specs=vmem,
         scratch_shapes=[
             pltpu.VMEM((HD, tokens), jnp.bfloat16),
-            pltpu.VMEM((HD, tokens), jnp.bfloat16),
-            pltpu.VMEM((HD, tokens), jnp.bfloat16),
-            pltpu.VMEM((tokens, HD), jnp.bfloat16),
-            pltpu.VMEM((tokens, HD), jnp.bfloat16),
+            pltpu.VMEM((slots + tokens, HD), jnp.bfloat16),
+            pltpu.VMEM((HD, slots + tokens), jnp.bfloat16),
         ],
-        compiler_params=pltpu.CompilerParams(vmem_limit_bytes=32 << 20),
+        compiler_params=pltpu.CompilerParams(vmem_limit_bytes=48 << 20),
         name="attend",
-    )(lengths, groups, info, x, sk, sv)
-
-
-def to_tokens_kernel(n, x, out, send_sem, recv_sem, local_sem):
+    )(lengths, groups, one, two, sk, sv)
+
+
+def project_kernel(n, x, w, out, *scratch):
+    landed, w_v, turned, sent, came = scratch[:5]
+    send_sem, recv_sem, local_sem, w_sem, over_sem, back_sem = scratch[5:]
     me = lax.axis_index("seq")
-    greet(me, n)
-    exchange(me, n, x, out, send_sem, recv_sem, local_sem)
-
-
-def to_tokens(x):
-    n = x.shape[0]
+    mine = lax.axis_index("head")
+    other = 1 - mine
+    width, features = w.shape
+    half = features // 2
+    parts, piece, rows = sent.shape
+    loads = []
+    for number, side in enumerate((other, mine)):
+        at = pl.ds(pl.multiple_of(side * half, half), half)
+        loads.append(pltpu.make_async_copy(w.at[:, at], w_v.at[number], w_sem.at[number]))
+    greet(me, n, (other,))
+    for load in loads:
+        load.start()
+    greeted(n)
+    start, end = exchange(me, n, x, landed, send_sem, recv_sem, local_sem)
+    start()
+    end()
+    turned[...] = landed[...].reshape(width, rows).T
+
+    def share(number, j):
+        at = pl.ds(pl.multiple_of(j * piece, piece), piece)
+        return jnp.dot(
+            turned[...], w_v[number, :, at], preferred_element_type=jnp.float32
+        ).T
+
+    def over(j):
+        return pltpu.make_async_remote_copy(
+            src_ref=sent.at[j],
+            dst_ref=came.at[j],
+            send_sem=over_sem.at[j],
+            recv_sem=back_sem.at[j],
+            device_id={"head": other},
+            device_id_type=pl.DeviceIdType.MESH,
+        )
+
+    def theirs(j, carry):
+        sent[j] = share(0, j).astype(jnp.bfloat16)
+        over(j).start()
+        return carry
+
+    def ours(j, carry):
+        part = share(1, j)
+        over(j).wait()
+        at = pl.ds(pl.multiple_of(j * piece, piece), piece)
+        out[at, :] = (part + came[j].astype(jnp.float32)).astype(jnp.bfloat16)
+        return carry
+
+    loads[0].wait()
+    lax.fori_loop(0, parts, theirs, 0)
+    loads[1].wait()
+    lax.fori_loop(0, parts, ours, 0)
+
+
+def project(x, w):
+    n, _, rows = x.shape
+    width, features = w.shape
+    half = features // 2
+    parts = half // TILE
     return pl.pallas_call(
-        functools.partial(to_tokens_kernel, n),
-        out_shape=jax.ShapeDtypeStruct(x.shape, x.dtype),
-        in_specs=[pl.BlockSpec(memory_space=pltpu.VMEM)],
-        out_specs=pl.BlockSpec(memory_space=pl.ANY),
+        functools.partial(project_kernel, n),
+        out_shape=jax.ShapeDtypeStruct((half, rows), x.dtype),
+        in_specs=[pl.BlockSpec(memory_space=pltpu.VMEM), pl.BlockSpec(memory_space=pl.ANY)],
+        out_specs=pl.BlockSpec(memory_space=pltpu.VMEM),
         scratch_shapes=[
+            pltpu.VMEM(x.shape, jnp.bfloat16),
+            pltpu.VMEM((2, width, half), jnp.bfloat16),
+            pltpu.VMEM((rows, width), jnp.bfloat16),
+            pltpu.VMEM((parts, TILE, rows), jnp.bfloat16),
+            pltpu.VMEM((parts, TILE, rows), jnp.bfloat16),
             pltpu.SemaphoreType.DMA((n,)),
             pltpu.SemaphoreType.DMA((n,)),
             pltpu.SemaphoreType.DMA,
+            pltpu.SemaphoreType.DMA((2,)),
+            pltpu.SemaphoreType.DMA((parts,)),
+            pltpu.SemaphoreType.DMA((parts,)),
         ],
-        compiler_params=pltpu.CompilerParams(collective_id=1, has_side_effects=True),
-        name="to_tokens",
-    )(x)
+        compiler_params=pltpu.CompilerParams(
+            collective_id=1, has_side_effects=True, vmem_limit_bytes=48 << 20
+        ),
+        name="project",
+    )(x, w)
 
 
 def by_heads(
     queries, keys, values, cache_k, cache_v, sink_k, sink_v, suffix_lengths, request_group, w_out
 ):
     n = lax.axis_size("seq")
-    rows, width = queries.shape
-    starts = starts_of(suffix_lengths)
-    index = jnp.arange(n * rows, dtype=jnp.int32)
-    inside = (starts[:, None] <= index[None, :]) & (
-        index[None, :] < (starts + suffix_lengths)[:, None]
-    )
-    info = jnp.stack(
-        [
-            jnp.sum(jnp.where(inside, starts[:, None], 0), axis=0),
-            jnp.sum(jnp.where(inside, request_group[:, None], 0), axis=0),
-        ]
-    )
     me = lax.axis_index("seq")
     sk = lax.dynamic_slice_in_dim(sink_k, me * HD, HD, 1)
     sv = lax.dynamic_slice_in_dim(sink_v, me * HD, HD, 1).T
-    x = to_heads(n, queries, keys, values, cache_k, cache_v)
-    attn = attend(x, sk, sv, suffix_lengths, request_group, info)
-    attn = to_tokens(attn).reshape(width, rows)
-    return lax.psum_scatter(
-        jnp.einsum("cd,cs->ds", w_out, attn, preferred_element_type=jnp.float32).astype(
-            jnp.bfloat16
-        ),
-        "head",
-        scatter_dimension=0,
-        tiled=True,
-    )
+    one, two = to_heads(n, queries, keys, values, cache_k, cache_v)
+    attn = attend(one, two, sk, sv, suffix_lengths, request_group)
+    return project(attn, w_out)
 
 
 def shards(queries, keys, values, cache_k, *rest):
@@ -365,6 +458,8 @@
         and TILE % rows == 0
         and cache_k.shape[0] == rows
         and (n * rows) % W == 0
+        and lax.axis_size("head") == 2
+        and rest[-1].shape[1] % (2 * TILE) == 0
     )
     return (by_heads if fits else gathered)(queries, keys, values, cache_k, *rest)
 

time: 141 us -> 99.4 us (0.70)
  waiting for transfers between devices: 20.5 us -> 0 us
  between operations: 13.5 us -> 0.04 us
  matrix products: 6.13 us -> 0 us
  Pallas kernels: 87.6 us -> 91.3 us
  other arithmetic: 2.23 us -> 0 us
  local copies, waits for them, and re-layouts: 9.82 us -> 7.92 us
    reduce_scatter x1 -> x0, waiting for transfers between devices: 20.5 us -> none  [by_heads(): lax.psum_scatter(jnp.einsum('cd,cs->ds', w_out, attn, preferred_element_t...]
    dot_general x1 -> x0, matrix products: 6.13 us -> none  [by_heads(): jnp.einsum('cd,cs->ds', w_out, attn, preferred_element_type=jnp.float32)]
    pallas_call x3, Pallas kernels: 87.6 us -> 91.3 us  [the longest x1 44.4 us: to_heads(): pl.pallas_call(functools.partial(to_heads_kernel, n), out_shape=[jax.Shap...]
    reduce_scatter x1 -> x0, local copies, waits for them, and re-layouts: 1.91 us -> none  [by_heads(): lax.psum_scatter(jnp.einsum('cd,cs->ds', w_out, attn, preferred_element_t...]
    reduce_sum x2 -> x0, other arithmetic: 1.55 us -> none  [the longest x1 0.78 us: by_heads(): jnp.sum(jnp.where(inside, starts[:, None], 0), axis=0)]
    unnamed x17 -> x16, local copies, waits for them, and re-layouts: 7.13 us -> 7.14 us
  transfers between devices with their start and end apart: 1 -> 0, of which waited for: 1 -> 0; matrix products, arithmetic and copies ran while one was open for 0% -> 0% of each run, Pallas kernels for 0% -> 0%
where the time goes in v2:
time: 99.4 us; the launch traced here: 99.3 us
  Pallas kernels  91.3 us (92%)
  local copies, waits for them, and re-layouts  7.92 us (8%)
    pallas_call x1, Pallas kernels, to_heads(): pl.pallas_call(functools.partial(to_heads_kernel, n), out_shape=[jax.Shap...  44.4 us
    pallas_call x1, Pallas kernels, project(): pl.pallas_call(functools.partial(project_kernel, n), out_shape=jax.ShapeD...  28.5 us
    pallas_call x1, Pallas kernels, attend(): pl.pallas_call(functools.partial(attend_kernel, tokens, slots), out_shape...  18.4 us
    unnamed x16, local copies, waits for them, and re-layouts  7.14 us

profile of v2, /device:TPU:0, one launch (start us, length us, event | category | flops | bytes accessed | tf_op | source)
XLA Modules:
  0.0 99.3 jit_solution(15161493222474325750)
XLA Ops:
  0.0 0.8 constant_dynamic-slice_fusion
  0.8 0.1 copy.12
  0.9 0.0 copy-start
  0.9 1.0 %copy-done = bf16[128,1536]{1,0:T(8,128)(2,1)S(1)} copy-done((bf16[128,1536]{1,0:T(8,128)(2,1)S(1)}, bf16[128,1536]{1,0:T(8,128)(2,1)}, u32[]{:S(2)}) %copy-start) | copy-done | bytes 393240
  1.9 0.0 copy-start.1
  1.9 1.0 %copy-done.1 = bf16[128,1536]{1,0:T(8,128)(2,1)S(1)} copy-done((bf16[128,1536]{1,0:T(8,128)(2,1)S(1)}, bf16[128,1536]{1,0:T(8,128)(2,1)}, u32[]{:S(2)}) %copy-start.1) | copy-done | bytes 393240
  2.9 0.0 copy-start.2
  2.9 1.0 %copy-done.2 = bf16[128,1536]{1,0:T(8,128)(2,1)S(1)} copy-done((bf16[128,1536]{1,0:T(8,128)(2,1)S(1)}, bf16[128,1536]{1,0:T(8,128)(2,1)}, u32[]{:S(2)}) %copy-start.2) | copy-done | bytes 393240
  3.9 0.0 copy-start.3
  3.9 1.0 %copy-done.3 = bf16[128,1536]{1,0:T(8,128)(2,1)S(1)} copy-done((bf16[128,1536]{1,0:T(8,128)(2,1)S(1)}, bf16[128,1536]{1,0:T(8,128)(2,1)}, u32[]{:S(2)}) %copy-start.3) | copy-done | bytes 393240
  4.9 0.0 copy-start.4
  4.9 1.0 %copy-done.4 = bf16[128,1536]{1,0:T(8,128)(2,1)S(1)} copy-done((bf16[128,1536]{1,0:T(8,128)(2,1)S(1)}, bf16[128,1536]{1,0:T(8,128)(2,1)}, u32[]{:S(2)}) %copy-start.4) | copy-done | bytes 393240
  5.9 44.4 %to_heads.1 = (bf16[16,3,96,128]{3,2,1,0:T(8,128)(2,1)S(1)}, bf16[16,2,96,128]{3,2,1,0:T(8,128)(2,1)S(1)}) custom-call(bf16[128,1536]{1,0:T(8,128)(2,1)S(1)} %copy-done, bf16[128,1536]{1,0:T(8,128)(2,1)S(1)} %copy-done.1, bf16[128,1536]{1,0:T(8,128)(2,1)S(1)} %copy-done.2, bf16[128,1536]{1,0:T(8,128)(2,1)S(1)} %copy-done.3, bf16[128,1536]{1,0:T(8,128)(2,1)S(1)} %copy-done.4), custom_call_target="tpu_custom_call" | custom-call | tf_op jit(solution)/shard_map/to_heads/pallas_call | solution.py:207
  50.3 0.0 copy-start.5
  50.3 0.6 copy-done.5
  50.9 0.0 copy-start.6
  50.9 0.7 copy-done.6
  51.6 18.4 %attend.1.x = bf16[16,96,128]{2,1,0:T(8,128)(2,1)S(1)} custom-call(s32[4]{0:T(128)S(1)} %copy-done.5, s32[4]{0:T(128)S(1)} %copy-done.6, bf16[16,3,96,128]{3,2,1,0:T(8,128)(2,1)S(1)} %get-tuple-element.7.one, bf16[16,2,96,128]{3,2,1,0:T(8,128)(2,1)S(1)} %get-tuple-element.8.two, bf16[8,96]{1,0:T(8,128)(2,1)S(1)} %get-tuple-element.10.sk, ...), custom_call_target="tpu_custom_call" | custom-call | tf_op jit(solution)/shard_map/attend/pallas_call | solution.py:338
  70.0 28.5 %project.1 = bf16[1536,128]{1,0:T(8,128)(2,1)S(1)} custom-call(bf16[16,96,128]{2,1,0:T(8,128)(2,1)S(1)} %attend.1.x, bf16[1536,3072]{1,0:T(8,128)(2,1)} %w.1), custom_call_target="tpu_custom_call" | custom-call | tf_op jit(solution)/shard_map/project/pallas_call | solution.py:414
  98.5 0.7 copy.14
Async XLA Ops:
  0.9 1.0 %copy-start = (bf16[128,1536]{1,0:T(8,128)(2,1)S(1)}, bf16[128,1536]{1,0:T(8,128)(2,1)}, u32[]{:S(2)}) copy-start(bf16[128,1536]{1,0:T(8,128)(2,1)} %refs_0_.1) | copy-start | bytes 1179652
  1.9 1.0 %copy-start.1 = (bf16[128,1536]{1,0:T(8,128)(2,1)S(1)}, bf16[128,1536]{1,0:T(8,128)(2,1)}, u32[]{:S(2)}) copy-start(bf16[128,1536]{1,0:T(8,128)(2,1)} %refs_1_.1) | copy-start | bytes 1179652
  2.9 1.0 %copy-start.2 = (bf16[128,1536]{1,0:T(8,128)(2,1)S(1)}, bf16[128,1536]{1,0:T(8,128)(2,1)}, u32[]{:S(2)}) copy-start(bf16[128,1536]{1,0:T(8,128)(2,1)} %refs_2_.1) | copy-start | bytes 1179652
  3.9 1.0 %copy-start.3 = (bf16[128,1536]{1,0:T(8,128)(2,1)S(1)}, bf16[128,1536]{1,0:T(8,128)(2,1)}, u32[]{:S(2)}) copy-start(bf16[128,1536]{1,0:T(8,128)(2,1)} %refs_3_.1) | copy-start | bytes 1179652
  4.9 1.0 %copy-start.4 = (bf16[128,1536]{1,0:T(8,128)(2,1)S(1)}, bf16[128,1536]{1,0:T(8,128)(2,1)}, u32[]{:S(2)}) copy-start(bf16[128,1536]{1,0:T(8,128)(2,1)} %refs_4_.1) | copy-start | bytes 1179652
  50.3 0.7 copy-start.5
  50.9 0.7 copy-start.6

commit v3 on v2

--- a/solution.py
+++ b/solution.py
@@ -171,10 +171,56 @@
     return start, end
 
 
-def to_heads_kernel(n, *refs):
-    five, (first, second), refs = refs[:5], refs[5:7], refs[7:]
-    raw, stage_one, stage_two, load_sem, send_sem, recv_sem, local_sem = refs
+def pipelined(total, q_tile, key_rows, value_columns, limits, state):
+    factor = math.log2(math.e) / math.sqrt(HD)
+    column = lax.broadcasted_iota(jnp.int32, (TILE, 1), 0)
+
+    def scores(t):
+        return jnp.dot(key_rows(t), q_tile, preferred_element_type=jnp.float32)
+
+    def weigh(t, prob):
+        return jnp.dot(value_columns(t), prob, preferred_element_type=jnp.float32)
+
+    def step(t, state):
+        top, den, acc, score, prob = state
+        following = scores(jnp.minimum(t + 1, total - 1))
+        acc = acc + weigh(jnp.maximum(t - 1, 0), prob)
+        at, low, high = limits(t)
+        index_k = at + column
+        seen = index_k > low
+        if high is not None:
+            seen = seen & (index_k <= high)
+        score = jnp.where(seen, score, jnp.float32(-1e30))
+        new_top = jnp.maximum(top, jnp.max(score, axis=0, keepdims=True))
+        shrink = jnp.exp2((top - new_top) * factor)
+        prob = jnp.exp2((score - new_top) * factor)
+        den = den * shrink + jnp.sum(prob, axis=0, keepdims=True)
+        return new_top, den, acc * shrink, following, prob.astype(jnp.bfloat16)
+
+    state = (*state, scores(0), jnp.zeros((TILE, TILE), jnp.bfloat16))
+    top, den, acc, _, prob = lax.fori_loop(0, total, step, state)
+    return top, den, acc + weigh(total - 1, prob)
+
+
+def facts(first, lengths, groups):
+    index_q = first + lax.broadcasted_iota(jnp.int32, (1, TILE), 1)
+    begin = jnp.int32(0)
+    start_q = jnp.zeros((1, TILE), jnp.int32)
+    group_q = jnp.zeros((1, TILE), jnp.int32)
+    for r in range(lengths.shape[0]):
+        inside = index_q >= begin
+        start_q = jnp.where(inside, begin, start_q)
+        group_q = jnp.where(inside, groups[r], group_q)
+        begin = begin + lengths[r]
+    return index_q, start_q, group_q
+
+
+def to_heads_kernel(n, lengths, groups, sk, sv, *refs):
+    five, (second, q_t, tops, dens, accs), refs = refs[:5], refs[5:10], refs[10:]
+    raw, stage_one, stage_two, first, k_n, v_t, load_sem, send_sem, recv_sem, local_sem = refs
     me = lax.axis_index("seq")
+    rows = five[0].shape[0]
+    tokens = n * rows
     loads = [pltpu.make_async_copy(five[a], raw.at[a], load_sem.at[a]) for a in range(5)]
     for load in loads:
         load.start()
@@ -196,132 +242,137 @@
         )
         start()
         ends.append(end)
-    for end in ends:
-        end()
-
-
-def to_heads(n, *arrays):
+
+    ends[0]()
+    for b in range(n):
+        at = pl.ds(b * rows, rows)
+        q_t[:, at] = first[b, 0]
+        k_n[at, :] = first[b, 1].T
+        v_t[:, at] = first[b, 2]
+    factor = math.log2(math.e) / math.sqrt(HD)
+    sink_column = lax.broadcasted_iota(jnp.int32, (sk.shape[0], 1), 0) // SINKS
+
+    def tile(i, carry):
+        here = pl.ds(pl.multiple_of(i * TILE, TILE), TILE)
+        index_q, start_q, group_q = facts(i * TILE, lengths, groups)
+        q_tile = q_t[:, here]
+        score = jnp.dot(sk[...], q_tile, preferred_element_type=jnp.float32)
+        score = jnp.where(sink_column == group_q, score, jnp.float32(-1e30))
+        top = jnp.max(score, axis=0, keepdims=True)
+        prob = jnp.exp2((score - top) * factor)
+        den = jnp.sum(prob, axis=0, keepdims=True)
+        acc = jnp.dot(sv[...], prob.astype(jnp.bfloat16), preferred_element_type=jnp.float32)
+        begin = jnp.maximum(i - W // TILE, 0)
+
+        def chunk(t):
+            return pl.multiple_of((begin + t) * TILE, TILE)
+
+        top, den, acc = pipelined(
+            i + 1 - begin,
+            q_tile,
+            lambda t: k_n[pl.ds(chunk(t), TILE), :],
+            lambda t: v_t[:, pl.ds(chunk(t), TILE)],
+            lambda t: (chunk(t), start_q - 1, index_q),
+            (top, den, acc),
+        )
+        tops[:, here] = top
+        dens[:, here] = den
+        accs[:, here] = acc
+        return carry
+
+    lax.fori_loop(0, tokens // TILE, tile, 0)
+    ends[1]()
+
+
+def to_heads(n, lengths, groups, sk, sv, *arrays):
     rows, width = arrays[0].shape
+    tokens = n * rows
     shapes = [(n, 3, HD, rows), (n, 2, HD, rows)]
     anywhere = pl.BlockSpec(memory_space=pl.ANY)
+    vmem = pl.BlockSpec(memory_space=pltpu.VMEM)
+    smem = pl.BlockSpec(memory_space=pltpu.SMEM)
     return pl.pallas_call(
         functools.partial(to_heads_kernel, n),
-        out_shape=[jax.ShapeDtypeStruct(shape, jnp.bfloat16) for shape in shapes],
-        in_specs=[anywhere] * 5,
-        out_specs=[anywhere] * 2,
+        out_shape=[
+            jax.ShapeDtypeStruct(shapes[1], jnp.bfloat16),
+            jax.ShapeDtypeStruct((HD, tokens), jnp.bfloat16),
+            jax.ShapeDtypeStruct((1, tokens), jnp.float32),
+            jax.ShapeDtypeStruct((1, tokens), jnp.float32),
+            jax.ShapeDtypeStruct((HD, tokens), jnp.float32),
+        ],
+        in_specs=[smem, smem, vmem, vmem] + [anywhere] * 5,
+        out_specs=[anywhere] + [vmem] * 4,
         scratch_shapes=[
             pltpu.VMEM((5, rows, width), jnp.bfloat16),
             pltpu.VMEM(shapes[0], jnp.bfloat16),
             pltpu.VMEM(shapes[1], jnp.bfloat16),
+            pltpu.VMEM(shapes[0], jnp.bfloat16),
+            pltpu.VMEM((tokens, HD), jnp.bfloat16),
+            pltpu.VMEM((HD, tokens), jnp.bfloat16),
             pltpu.SemaphoreType.DMA((5,)),
             pltpu.SemaphoreType.DMA((2, n)),
             pltpu.SemaphoreType.DMA((2, n)),
             pltpu.SemaphoreType.DMA((2,)),
         ],
         compiler_params=pltpu.CompilerParams(
-            collective_id=0, has_side_effects=True, vmem_limit_bytes=48 << 20
+            collective_id=0, has_side_effects=True, vmem_limit_bytes=62 << 20
         ),
         name="to_heads",
-    )(*arrays)
-
-
-def attend_kernel(tokens, slots, lengths, groups, one, two, sk, sv, out, q_t, k_n, v_t):
-    n, _, _, rows = one.shape
-    count = lengths.shape[0]
+    )(lengths, groups, sk, sv, *arrays)
+
+
+def attend_kernel(tokens, slots, lengths, groups, two, q_t, tops, dens, accs, out, k_n, v_t):
+    n, _, _, rows = two.shape
     own = slots // W
-    factor = math.log2(math.e) / math.sqrt(HD)
+    per = W // TILE
     for b in range(n):
         at = pl.ds(b * rows, rows)
-        later = pl.ds(slots + b * rows, rows)
-        q_t[:, at] = one[b, 0]
-        k_n[later, :] = one[b, 1].T
-        v_t[:, later] = one[b, 2]
         k_n[at, :] = two[b, 0].T
         v_t[:, at] = two[b, 1]
-    column = lax.broadcasted_iota(jnp.int32, (TILE, 1), 0)
-    sink_column = lax.broadcasted_iota(jnp.int32, (sk.shape[0], 1), 0) // SINKS
-    far = jnp.int32(1 << 30)
 
     def tile(i, carry):
         first = i * TILE
         last = first + TILE
-        index_q = first + lax.broadcasted_iota(jnp.int32, (1, TILE), 1)
+        index_q, start_q, group_q = facts(first, lengths, groups)
         begin = jnp.int32(0)
-        earliest = first
-        lowest = [jnp.int32(W) for _ in range(own)]
-        start_q = jnp.zeros((1, TILE), jnp.int32)
-        group_q = jnp.zeros((1, TILE), jnp.int32)
-        for r in range(count):
+        lowest = [jnp.int32(W - 1) for _ in range(own)]
+        for r in range(lengths.shape[0]):
             end = begin + lengths[r]
             low = jnp.maximum(first, begin)
             touches = low < jnp.minimum(last, end)
-            earliest = jnp.where(touches, jnp.minimum(earliest, begin), earliest)
             for g in range(own):
                 lowest[g] = jnp.where(
                     touches & (groups[r] == g), jnp.minimum(lowest[g], low - begin), lowest[g]
                 )
-            inside = index_q >= begin
-            start_q = jnp.where(inside, begin, start_q)
-            group_q = jnp.where(inside, groups[r], group_q)
             begin = end
         offset_q = index_q - start_q
         sections = []
         for g in range(own):
             chunk = (lowest[g] + 1) // TILE
             limit = g * W + jnp.where(group_q == g, offset_q, jnp.int32(W))
-            sections.append(
-                (g * (W // TILE) + chunk, W // TILE - chunk, limit, jnp.zeros_like(limit) + far)
-            )
-        chunk = earliest // TILE
-        sections.append(
-            (slots // TILE + chunk, i + 1 - chunk, slots + start_q - 1, slots + index_q)
-        )
+            sections.append((g * per + chunk, per - chunk, limit))
         total = sum(section[1] for section in sections)
 
         def find(t):
-            chunk, low, high = sections[0][0] + t, sections[0][2], sections[0][3]
+            chunk, low = sections[0][0] + t, sections[0][2]
             before = sections[0][1]
-            for begins, number, lower, upper in sections[1:]:
+            for begins, number, lower in sections[1:]:
                 here = t >= before
                 chunk = jnp.where(here, begins + t - before, chunk)
                 low = jnp.where(here, lower, low)
-                high = jnp.where(here, upper, high)
                 before = before + number
-            return pl.multiple_of(chunk * TILE, TILE), low, high
-
-        q_tile = q_t[:, pl.ds(pl.multiple_of(first, TILE), TILE)]
-
-        def scores(t):
-            at, _, _ = find(t)
-            return jnp.dot(k_n[pl.ds(at, TILE), :], q_tile, preferred_element_type=jnp.float32)
-
-        def weigh(t, prob):
-            at, _, _ = find(t)
-            return jnp.dot(v_t[:, pl.ds(at, TILE)], prob, preferred_element_type=jnp.float32)
-
-        score = jnp.dot(sk[...], q_tile, preferred_element_type=jnp.float32)
-        score = jnp.where(sink_column == group_q, score, jnp.float32(-1e30))
-        top = jnp.max(score, axis=0, keepdims=True)
-        prob = jnp.exp2((score - top) * factor)
-        den = jnp.sum(prob, axis=0, keepdims=True)
-        acc = jnp.dot(sv[...], prob.astype(jnp.bfloat16), preferred_element_type=jnp.float32)
-
-        def step(t, state):
-            top, den, acc, score, prob = state
-            following = scores(jnp.minimum(t + 1, total - 1))
-            acc = acc + weigh(jnp.maximum(t - 1, 0), prob)
-            at, low, high = find(t)
-            index_k = at + column
-            score = jnp.where((index_k > low) & (index_k <= high), score, jnp.float32(-1e30))
-            new_top = jnp.maximum(top, jnp.max(score, axis=0, keepdims=True))
-            shrink = jnp.exp2((top - new_top) * factor)
-            prob = jnp.exp2((score - new_top) * factor)
-            den = den * shrink + jnp.sum(prob, axis=0, keepdims=True)
-            return new_top, den, acc * shrink, following, prob.astype(jnp.bfloat16)
-
-        state = (top, den, acc, scores(0), jnp.zeros((TILE, TILE), jnp.bfloat16))
-        top, den, acc, score, prob = lax.fori_loop(0, total, step, state)
-        acc = acc + weigh(total - 1, prob)
+            chunk = jnp.clip(chunk, 0, own * per - 1)
+            return pl.multiple_of(chunk * TILE, TILE), low, None
+
+        here = pl.ds(pl.multiple_of(first, TILE), TILE)
+        top, den, acc = pipelined(
+            total,
+            q_t[:, here],
+            lambda t: k_n[pl.ds(find(t)[0], TILE), :],
+            lambda t: v_t[:, pl.ds(find(t)[0], TILE)],
+            find,
+            (tops[:, here], dens[:, here], accs[:, here]),
+        )
         result = (acc / den).astype(jnp.bfloat16)
         for part in range(TILE // rows):
             out[i * (TILE // rows) + part] = result[:, part * rows : (part + 1) * rows]
@@ -330,24 +381,23 @@
     lax.fori_loop(0, tokens // TILE, tile, 0)
 
 
-def attend(one, two, sk, sv, lengths, groups):
-    n, _, _, rows = one.shape
+def attend(lengths, groups, two, q_t, tops, dens, accs):
+    n, _, _, rows = two.shape
     tokens = slots = n * rows
     vmem = pl.BlockSpec(memory_space=pltpu.VMEM)
     smem = pl.BlockSpec(memory_space=pltpu.SMEM)
     return pl.pallas_call(
         functools.partial(attend_kernel, tokens, slots),
         out_shape=jax.ShapeDtypeStruct((n, HD, rows), jnp.bfloat16),
-        in_specs=[smem, smem, vmem, vmem, vmem, vmem],
+        in_specs=[smem, smem] + [vmem] * 5,
         out_specs=vmem,
         scratch_shapes=[
-            pltpu.VMEM((HD, tokens), jnp.bfloat16),
-            pltpu.VMEM((slots + tokens, HD), jnp.bfloat16),
-            pltpu.VMEM((HD, slots + tokens), jnp.bfloat16),
+            pltpu.VMEM((slots, HD), jnp.bfloat16),
+            pltpu.VMEM((HD, slots), jnp.bfloat16),
         ],
         compiler_params=pltpu.CompilerParams(vmem_limit_bytes=48 << 20),
         name="attend",
-    )(lengths, groups, one, two, sk, sv)
+    )(lengths, groups, two, q_t, tops, dens, accs)
 
 
 def project_kernel(n, x, w, out, *scratch):
@@ -443,8 +493,19 @@
     me = lax.axis_index("seq")
     sk = lax.dynamic_slice_in_dim(sink_k, me * HD, HD, 1)
     sv = lax.dynamic_slice_in_dim(sink_v, me * HD, HD, 1).T
-    one, two = to_heads(n, queries, keys, values, cache_k, cache_v)
-    attn = attend(one, two, sk, sv, suffix_lengths, request_group)
+    two, *state = to_heads(
+        n,
+        suffix_lengths,
+        request_group,
+        sk,
+        sv,
+        queries,
+        keys,
+        values,
+        cache_k,
+        cache_v,
+    )
+    attn = attend(suffix_lengths, request_group, two, *state)
     return project(attn, w_out)
 
 

time: 99.4 us -> 98.5 us (level)
  Pallas kernels: 91.3 us -> 88.8 us
    pallas_call x1, Pallas kernels: 18.4 us -> 10.7 us  [attend(): pl.pallas_call(functools.partial(attend_kernel, tokens, slots), out_shape...]
    pallas_call x1, Pallas kernels: 28.5 us -> 32.4 us  [project(): pl.pallas_call(functools.partial(project_kernel, n), out_shape=jax.ShapeD...]
    pallas_call x1, Pallas kernels: 44.4 us -> 45.7 us  [to_heads(): pl.pallas_call(functools.partial(to_heads_kernel, n), out_shape=[jax.Shap...]
where the time goes in v3:
time: 98.5 us; the launch traced here: 97.6 us
  Pallas kernels  88.8 us (90%)
  local copies, waits for them, and re-layouts  8.78 us (9%)
    pallas_call x1, Pallas kernels, to_heads(): pl.pallas_call(functools.partial(to_heads_kernel, n), out_shape=[jax.Shap...  45.7 us
    pallas_call x1, Pallas kernels, project(): pl.pallas_call(functools.partial(project_kernel, n), out_shape=jax.ShapeD...  32.4 us
    pallas_call x1, Pallas kernels, attend(): pl.pallas_call(functools.partial(attend_kernel, tokens, slots), out_shape...  10.7 us
    unnamed x16, local copies, waits for them, and re-layouts  7.41 us

profile of v3, /device:TPU:0, one launch (start us, length us, event | category | flops | bytes accessed | tf_op | source)
XLA Modules:
  0.0 97.6 jit_solution(6144048657227426049)
XLA Ops:
  0.0 1.4 %constant_dynamic-slice_fusion = (bf16[8,96]{1,0:T(8,128)(2,1)S(1)}, bf16[8,96]{1,0:T(8,128)(2,1)}) fusion(bf16[8,1536]{1,0:T(8,128)(2,1)} %param.16, s32[]{:T(128)S(6)} %select_n.4, bf16[8,1536]{1,0:T(8,128)(2,1)} %param.15), kind=kLoop, calls=%fused_computation | loop fusion | bytes 6148 | tf_op jit(solution)/shard_map/dynamic_slice | solution.py:495
  1.4 0.7 copy.12
  2.1 45.7 %to_heads.1 = (bf16[16,2,96,128]{3,2,1,0:T(8,128)(2,1)}, bf16[96,2048]{1,0:T(8,128)(2,1)}, f32[1,2048]{1,0:T(1,128)}, f32[1,2048]{1,0:T(1,128)}, f32[96,2048]{1,0:T(8,128)}) custom-call(s32[4]{0:T(128)} %lengths.3, s32[4]{0:T(128)} %groups.3, bf16[8,96]{1,0:T(8,128)(2,1)} %get-tuple-element.16.sk, bf16[96,8]{1,0:T(8,128)(2,1)} %bitcast.1, ...), custom_call_target="tpu_custom_call" | custom-call | tf_op jit(solution)/shard_map/to_heads/pallas_call | solution.py:294
  47.8 0.0 copy-start
  47.8 1.1 %copy-done = bf16[16,2,96,128]{3,2,1,0:T(8,128)(2,1)S(1)} copy-done((bf16[16,2,96,128]{3,2,1,0:T(8,128)(2,1)S(1)}, bf16[16,2,96,128]{3,2,1,0:T(8,128)(2,1)}, u32[]{:S(2)}) %copy-start) | copy-done | bytes 786456
  48.9 0.0 copy-start.1
  48.9 1.1 %copy-done.1 = f32[96,2048]{1,0:T(8,128)S(1)} copy-done((f32[96,2048]{1,0:T(8,128)S(1)}, f32[96,2048]{1,0:T(8,128)}, u32[]{:S(2)}) %copy-start.1) | copy-done | bytes 786456
  50.0 0.0 copy-start.2
  50.0 1.0 %copy-done.2 = bf16[96,2048]{1,0:T(8,128)(2,1)S(1)} copy-done((bf16[96,2048]{1,0:T(8,128)(2,1)S(1)}, bf16[96,2048]{1,0:T(8,128)(2,1)}, u32[]{:S(2)}) %copy-start.2) | copy-done | bytes 393240
  51.0 0.0 copy-start.3
  51.0 0.7 copy-done.3
  51.7 0.0 copy-start.4
  51.7 0.7 copy-done.4
  52.4 0.0 copy-start.5
  52.4 0.7 copy-done.5
  53.1 0.0 copy-start.6
  53.1 0.7 copy-done.6
  53.7 10.7 %attend.1.x = bf16[16,96,128]{2,1,0:T(8,128)(2,1)S(1)} custom-call(s32[4]{0:T(128)S(1)} %copy-done.5, s32[4]{0:T(128)S(1)} %copy-done.6, bf16[16,2,96,128]{3,2,1,0:T(8,128)(2,1)S(1)} %copy-done, bf16[96,2048]{1,0:T(8,128)(2,1)S(1)} %copy-done.2, f32[1,2048]{1,0:T(1,128)S(1)} %copy-done.3, f32[1,2048]{1,0:T(1,128)S(1)} %copy-done.4, f32[96,2048]{1,0:T(8,128)S(1)} %copy-done.1), custom_call_target="tpu_custom_call" | custom-call | tf_op jit(solution)/shard_map/attend/pallas_call | solution.py:389
  64.4 32.4 %project.1 = bf16[1536,128]{1,0:T(8,128)(2,1)S(1)} custom-call(bf16[16,96,128]{2,1,0:T(8,128)(2,1)S(1)} %attend.1.x, bf16[1536,3072]{1,0:T(8,128)(2,1)} %w.1), custom_call_target="tpu_custom_call" | custom-call | tf_op jit(solution)/shard_map/project/pallas_call | solution.py:464
  96.9 0.7 copy.14
Async XLA Ops:
  47.8 1.1 %copy-start = (bf16[16,2,96,128]{3,2,1,0:T(8,128)(2,1)S(1)}, bf16[16,2,96,128]{3,2,1,0:T(8,128)(2,1)}, u32[]{:S(2)}) copy-start(bf16[16,2,96,128]{3,2,1,0:T(8,128)(2,1)} %get-tuple-element.10.two) | copy-start | bytes 2359300
  48.9 1.1 %copy-start.1 = (f32[96,2048]{1,0:T(8,128)S(1)}, f32[96,2048]{1,0:T(8,128)}, u32[]{:S(2)}) copy-start(f32[96,2048]{1,0:T(8,128)} %get-tuple-element.14.accs) | copy-start | bytes 2359300
  50.0 1.0 %copy-start.2 = (bf16[96,2048]{1,0:T(8,128)(2,1)S(1)}, bf16[96,2048]{1,0:T(8,128)(2,1)}, u32[]{:S(2)}) copy-start(bf16[96,2048]{1,0:T(8,128)(2,1)} %get-tuple-element.11.q_t) | copy-start | bytes 1179652
  51.0 0.7 copy-start.3
  51.7 0.7 copy-start.4
  52.4 0.7 copy-start.5
  53.1 0.7 copy-start.6

commit v4 on v3

--- a/solution.py
+++ b/solution.py
@@ -154,8 +154,12 @@
         copy_to(o).start()
         return carry
 
-    def one_end(o, carry):
-        copy_to(o).wait()
+    def one_sent(o, carry):
+        copy_to(o).wait_send()
+        return carry
+
+    def one_arrived(o, carry):
+        copy_to(o).wait_recv()
         return carry
 
     own = pltpu.make_async_copy(source.at[me], landing.at[me], local_sem)
@@ -164,11 +168,14 @@
         lax.fori_loop(1, n, one_start, 0)
         own.start()
 
-    def end():
-        lax.fori_loop(1, n, one_end, 0)
+    def sent():
+        lax.fori_loop(1, n, one_sent, 0)
+
+    def arrived():
+        lax.fori_loop(1, n, one_arrived, 0)
         own.wait()
 
-    return start, end
+    return start, sent, arrived
 
 
 def pipelined(total, q_tile, key_rows, value_columns, limits, state):
@@ -237,13 +244,15 @@
                     stage[4 * g + i, place] = turned[i * HD : (i + 1) * HD]
         if which == 0:
             greeted(n - 1)
-        start, end = exchange(
+        else:
+            ends[0][0]()
+        start, sent, arrived = exchange(
             me, n, stage, landing, send_sem.at[which], recv_sem.at[which], local_sem.at[which]
         )
         start()
-        ends.append(end)
-
-    ends[0]()
+        ends.append((sent, arrived))
+
+    ends[0][1]()
     for b in range(n):
         at = pl.ds(b * rows, rows)
         q_t[:, at] = first[b, 0]
@@ -261,7 +270,12 @@
         top = jnp.max(score, axis=0, keepdims=True)
         prob = jnp.exp2((score - top) * factor)
         den = jnp.sum(prob, axis=0, keepdims=True)
-        acc = jnp.dot(sv[...], prob.astype(jnp.bfloat16), preferred_element_type=jnp.float32)
+        acc = lax.dot_general(
+            sv[...],
+            prob.astype(jnp.bfloat16),
+            (((0,), (0,)), ((), ())),
+            preferred_element_type=jnp.float32,
+        )
         begin = jnp.maximum(i - W // TILE, 0)
 
         def chunk(t):
@@ -281,7 +295,8 @@
         return carry
 
     lax.fori_loop(0, tokens // TILE, tile, 0)
-    ends[1]()
+    ends[1][0]()
+    ends[1][1]()
 
 
 def to_heads(n, lengths, groups, sk, sv, *arrays):
@@ -395,7 +410,7 @@
             pltpu.VMEM((slots, HD), jnp.bfloat16),
             pltpu.VMEM((HD, slots), jnp.bfloat16),
         ],
-        compiler_params=pltpu.CompilerParams(vmem_limit_bytes=48 << 20),
+        compiler_params=pltpu.CompilerParams(vmem_limit_bytes=62 << 20),
         name="attend",
     )(lengths, groups, two, q_t, tops, dens, accs)
 
@@ -417,9 +432,9 @@
     for load in loads:
         load.start()
     greeted(n)
-    start, end = exchange(me, n, x, landed, send_sem, recv_sem, local_sem)
+    start, all_sent, arrived = exchange(me, n, x, landed, send_sem, recv_sem, local_sem)
     start()
-    end()
+    arrived()
     turned[...] = landed[...].reshape(width, rows).T
 
     def share(number, j):
@@ -454,6 +469,7 @@
     lax.fori_loop(0, parts, theirs, 0)
     loads[1].wait()
     lax.fori_loop(0, parts, ours, 0)
+    all_sent()
 
 
 def project(x, w):
@@ -480,7 +496,7 @@
             pltpu.SemaphoreType.DMA((parts,)),
         ],
         compiler_params=pltpu.CompilerParams(
-            collective_id=1, has_side_effects=True, vmem_limit_bytes=48 << 20
+            collective_id=1, has_side_effects=True, vmem_limit_bytes=62 << 20
         ),
         name="project",
     )(x, w)
@@ -492,7 +508,7 @@
     n = lax.axis_size("seq")
     me = lax.axis_index("seq")
     sk = lax.dynamic_slice_in_dim(sink_k, me * HD, HD, 1)
-    sv = lax.dynamic_slice_in_dim(sink_v, me * HD, HD, 1).T
+    sv = lax.dynamic_slice_in_dim(sink_v, me * HD, HD, 1)
     two, *state = to_heads(
         n,
         suffix_lengths,

time: 98.5 us -> 95.9 us (0.974)
  local copies, waits for them, and re-layouts: 8.78 us -> 3.13 us
  Pallas kernels: 88.8 us -> 92.5 us
    unnamed x16 -> x1, local copies, waits for them, and re-layouts: 7.41 us -> 1.77 us
    pallas_call x1, Pallas kernels: 45.7 us -> 49.7 us  [to_heads(): pl.pallas_call(functools.partial(to_heads_kernel, n), out_shape=[jax.Shap...]
    pallas_call x1, Pallas kernels: 32.4 us -> 29.6 us  [project(): pl.pallas_call(functools.partial(project_kernel, n), out_shape=jax.ShapeD...]
    pallas_call x1, Pallas kernels: 10.7 us -> 13.1 us  [attend(): pl.pallas_call(functools.partial(attend_kernel, tokens, slots), out_shape...]
where the time goes in v4:
time: 95.9 us; the launch traced here: 95.6 us
  Pallas kernels  92.5 us (96%)
  local copies, waits for them, and re-layouts  3.13 us (3%)
    pallas_call x1, Pallas kernels, to_heads(): pl.pallas_call(functools.partial(to_heads_kernel, n), out_shape=[jax.Shap...  49.7 us
    pallas_call x1, Pallas kernels, project(): pl.pallas_call(functools.partial(project_kernel, n), out_shape=jax.ShapeD...  29.6 us
    pallas_call x1, Pallas kernels, attend(): pl.pallas_call(functools.partial(attend_kernel, tokens, slots), out_shape...  13.1 us

profile of v4, /device:TPU:0, one launch (start us, length us, event | category | flops | bytes accessed | tf_op | source)
XLA Modules:
  0.0 95.6 jit_solution(12456223740477970993)
XLA Ops:
  0.0 1.4 %constant_dynamic-slice_fusion = (bf16[8,96]{1,0:T(8,128)(2,1)}, bf16[8,96]{1,0:T(8,128)(2,1)}) fusion(bf16[8,1536]{1,0:T(8,128)(2,1)} %param.16, s32[]{:T(128)S(6)} %select_n.4, bf16[8,1536]{1,0:T(8,128)(2,1)} %param.15), kind=kLoop, calls=%fused_computation | loop fusion | bytes 6148 | tf_op jit(solution)/shard_map/dynamic_slice | solution.py:511
  1.4 49.7 %to_heads.1 = (bf16[16,2,96,128]{3,2,1,0:T(8,128)(2,1)}, bf16[96,2048]{1,0:T(8,128)(2,1)}, f32[1,2048]{1,0:T(1,128)}, f32[1,2048]{1,0:T(1,128)}, f32[96,2048]{1,0:T(8,128)}) custom-call(s32[4]{0:T(128)} %lengths.3, s32[4]{0:T(128)} %groups.3, bf16[8,96]{1,0:T(8,128)(2,1)} %get-tuple-element.16.sk, bf16[8,96]{1,0:T(8,128)(2,1)} %get-tuple-element.15.sv, ...), custom_call_target="tpu_custom_call" | custom-call | tf_op jit(solution)/shard_map/to_heads/pallas_call | solution.py:309
  51.1 13.1 %attend.1.x = bf16[16,96,128]{2,1,0:T(8,128)(2,1)} custom-call(s32[4]{0:T(128)} %lengths.3, s32[4]{0:T(128)} %groups.3, bf16[16,2,96,128]{3,2,1,0:T(8,128)(2,1)} %get-tuple-element.10.two, bf16[96,2048]{1,0:T(8,128)(2,1)} %get-tuple-element.11.q_t, f32[1,2048]{1,0:T(1,128)} %get-tuple-element.12.tops, f32[1,2048]{1,0:T(1,128)} %get-tuple-element.13.dens, ...), custom_call_target="tpu_custom_call" | custom-call | tf_op jit(solution)/shard_map/attend/pallas_call | solution.py:404
  64.2 29.6 %project.1 = bf16[1536,128]{1,0:T(8,128)(2,1)} custom-call(bf16[16,96,128]{2,1,0:T(8,128)(2,1)} %attend.1.x, bf16[1536,3072]{1,0:T(8,128)(2,1)} %w.1), custom_call_target="tpu_custom_call" | custom-call | tf_op jit(solution)/shard_map/project/pallas_call | solution.py:480
  93.9 1.8 %copy.12 = bf16[1536,128]{1,0:T(8,128)(2,1)} copy(bf16[1536,128]{1,0:T(8,128)(2,1)} %project.1) | data formatting | bytes 786432

commit v5 on v4

--- a/solution.py
+++ b/solution.py
@@ -150,8 +150,8 @@
             device_id_type=pl.DeviceIdType.MESH,
         )
 
-    def one_start(o, carry):
-        copy_to(o).start()
+    def one_start(k, carry):
+        copy_to(n // 2 + (k + 1) // 2 * (1 - 2 * (k % 2))).start()
         return carry
 
     def one_sent(o, carry):
@@ -165,7 +165,7 @@
     own = pltpu.make_async_copy(source.at[me], landing.at[me], local_sem)
 
     def start():
-        lax.fori_loop(1, n, one_start, 0)
+        lax.fori_loop(0, n - 1, one_start, 0)
         own.start()
 
     def sent():
@@ -496,7 +496,7 @@
             pltpu.SemaphoreType.DMA((parts,)),
         ],
         compiler_params=pltpu.CompilerParams(
-            collective_id=1, has_side_effects=True, vmem_limit_bytes=62 << 20
+            collective_id=1, has_side_effects=True, vmem_limit_bytes=48 << 20
         ),
         name="project",
     )(x, w)

time: 95.9 us -> 94.3 us (0.983)
  Pallas kernels: 92.5 us -> 90.9 us
    pallas_call x1, Pallas kernels: 13.1 us -> 12 us  [attend(): pl.pallas_call(functools.partial(attend_kernel, tokens, slots), out_shape...]
where the time goes in v5:
time: 94.3 us; the launch traced here: 94 us
  Pallas kernels  90.9 us (96%)
  local copies, waits for them, and re-layouts  3.11 us (3%)
    pallas_call x1, Pallas kernels, to_heads(): pl.pallas_call(functools.partial(to_heads_kernel, n), out_shape=[jax.Shap...  49.8 us
    pallas_call x1, Pallas kernels, project(): pl.pallas_call(functools.partial(project_kernel, n), out_shape=jax.ShapeD...  29.1 us
    pallas_call x1, Pallas kernels, attend(): pl.pallas_call(functools.partial(attend_kernel, tokens, slots), out_shape...  12 us

profile of v5, /device:TPU:0, one launch (start us, length us, event | category | flops | bytes accessed | tf_op | source)
XLA Modules:
  0.0 94.0 jit_solution(4788392378786778252)
XLA Ops:
  0.0 1.4 %constant_dynamic-slice_fusion = (bf16[8,96]{1,0:T(8,128)(2,1)}, bf16[8,96]{1,0:T(8,128)(2,1)}) fusion(bf16[8,1536]{1,0:T(8,128)(2,1)} %param.16, s32[]{:T(128)S(6)} %select_n.4, bf16[8,1536]{1,0:T(8,128)(2,1)} %param.15), kind=kLoop, calls=%fused_computation | loop fusion | bytes 6148 | tf_op jit(solution)/shard_map/dynamic_slice | solution.py:511
  1.4 49.8 %to_heads.1 = (bf16[16,2,96,128]{3,2,1,0:T(8,128)(2,1)}, bf16[96,2048]{1,0:T(8,128)(2,1)}, f32[1,2048]{1,0:T(1,128)}, f32[1,2048]{1,0:T(1,128)}, f32[96,2048]{1,0:T(8,128)}) custom-call(s32[4]{0:T(128)} %lengths.3, s32[4]{0:T(128)} %groups.3, bf16[8,96]{1,0:T(8,128)(2,1)} %get-tuple-element.16.sk, bf16[8,96]{1,0:T(8,128)(2,1)} %get-tuple-element.15.sv, ...), custom_call_target="tpu_custom_call" | custom-call | tf_op jit(solution)/shard_map/to_heads/pallas_call | solution.py:309
  51.1 12.0 %attend.1.x = bf16[16,96,128]{2,1,0:T(8,128)(2,1)} custom-call(s32[4]{0:T(128)} %lengths.3, s32[4]{0:T(128)} %groups.3, bf16[16,2,96,128]{3,2,1,0:T(8,128)(2,1)} %get-tuple-element.10.two, bf16[96,2048]{1,0:T(8,128)(2,1)} %get-tuple-element.11.q_t, f32[1,2048]{1,0:T(1,128)} %get-tuple-element.12.tops, f32[1,2048]{1,0:T(1,128)} %get-tuple-element.13.dens, ...), custom_call_target="tpu_custom_call" | custom-call | tf_op jit(solution)/shard_map/attend/pallas_call | solution.py:404
  63.2 0.0 copy-start
  63.2 1.0 %copy-done = bf16[16,96,128]{2,1,0:T(8,128)(2,1)S(1)} copy-done((bf16[16,96,128]{2,1,0:T(8,128)(2,1)S(1)}, bf16[16,96,128]{2,1,0:T(8,128)(2,1)}, u32[]{:S(2)}) %copy-start) | copy-done | bytes 393240
  64.2 29.1 %project.1 = bf16[1536,128]{1,0:T(8,128)(2,1)S(1)} custom-call(bf16[16,96,128]{2,1,0:T(8,128)(2,1)S(1)} %copy-done, bf16[1536,3072]{1,0:T(8,128)(2,1)} %w.1), custom_call_target="tpu_custom_call" | custom-call | tf_op jit(solution)/shard_map/project/pallas_call | solution.py:480
  93.3 0.7 copy.12
Async XLA Ops:
  63.2 1.0 %copy-start = (bf16[16,96,128]{2,1,0:T(8,128)(2,1)S(1)}, bf16[16,96,128]{2,1,0:T(8,128)(2,1)}, u32[]{:S(2)}) copy-start(bf16[16,96,128]{2,1,0:T(8,128)(2,1)} %attend.1.x) | copy-start | bytes 1179652
